TPU v7x, 32 devices: a whole 2x2x4 slice. The times are simulated.
32 devices in a mesh: dp: 16 (over z, x, core), tensor: 2 (over y).
Axes of the slice: x: 2, y: 2, z: 4, core: 2. Of those that a mesh axis runs over, the one named last changes fastest.
Arguments:
- tokens: bfloat16 [8192, 8192], P('dp', 'tensor'), may hold values from -6 to 6
- cotangent: bfloat16 [8192, 1024], P('dp', 'tensor'), may hold values from -6 to 6
- frozen_key_weight: bfloat16 [8192, 1024], P(None, 'tensor'), may hold values from -0.0625 to 0.0625
- counts: int32 [16, 16], P('dp'), may hold values from 1 to 48, 512 in all within a row
- holder_assignment: int32 [16], replicated, may hold values from 0 to 15, each once
- adapter_down_matrix: float32 [16, 64, 8192], P('dp', None, 'tensor'), may hold values from -0.0625 to 0.0625
- adapter_up_matrix: float32 [16, 64, 1024], P('dp', None, 'tensor'), may hold values from -0.06 to 0.06
- down_first_moment: float32 [16, 64, 8192], P('dp', None, 'tensor'), may hold values from -12 to 12
- down_second_moment: float32 [16, 64, 8192], P('dp', None, 'tensor'), may hold values from 1 to 100
- up_first_moment: float32 [16, 64, 1024], P('dp', None, 'tensor'), may hold values from -30 to 30
- up_second_moment: float32 [16, 64, 1024], P('dp', None, 'tensor'), may hold values from 10 to 1000
Outputs:
- layer_out: bfloat16 [8192, 1024], P('dp', 'tensor')
- input_grad: bfloat16 [8192, 8192], P('dp', 'tensor')
- fresh_down_matrix: float32 [16, 64, 8192], P('dp', None, 'tensor')
- fresh_down_first: float32 [16, 64, 8192], P('dp', None, 'tensor')
- fresh_down_second: float32 [16, 64, 8192], P('dp', None, 'tensor')
- fresh_up_matrix: float32 [16, 64, 1024], P('dp', None, 'tensor')
- fresh_up_first: float32 [16, 64, 1024], P('dp', None, 'tensor')
- fresh_up_second: float32 [16, 64, 1024], P('dp', None, 'tensor')
Inputs may be any that keep to these rules, and one draw needn't show every extreme that they name: `counts`: row j gives, adapter by adapter in order, how many of dp index j's tokens belong to each adapter; dp index j's rows of tokens and cotangent are grouped in that order; each row sums to 512, and some entry of each row equals 48. A permutation: holder_assignment[a] is the dp index that holds adapter a.
All inputs are finite; a program needn't handle non-finite values.
Results may differ from a plain program's by a relative error of at most 0.0021.
Values may be sent and summed in bfloat16 or wider, within the bound.
A program may use at most 128 MiB of HBM per device.

v0:
```python
import jax
import jax.numpy as jnp
from jax import lax
from jax.sharding import PartitionSpec as P

adapter_scale = 2.0
learn_rate = 0.01
beta_one = 0.9
beta_two = 0.999
adam_eps = 1e-08
adam_step = 10


def optimizer_update(weight, moment, second, grad):
    moment_new = beta_one * moment + (1.0 - beta_one) * grad
    second_new = beta_two * second + (1.0 - beta_two) * grad * grad
    first_fix = 1.0 - beta_one**adam_step
    second_fix = 1.0 - beta_two**adam_step
    weight_new = weight - learn_rate * (moment_new / first_fix) / (
        jnp.sqrt(second_new / second_fix) + adam_eps
    )
    return (weight_new, moment_new, second_new)


def per_device(
    tokens,
    cotangent,
    frozen_key_weight,
    counts,
    holder_assignment,
    adapter_down_matrix,
    adapter_up_matrix,
    down_first_moment,
    down_second_moment,
    up_first_moment,
    up_second_moment,
):
    tok_rows = tokens.shape[0]
    feat_width = tokens.shape[1]
    key_width = cotangent.shape[1]
    adapter_rank_width = adapter_down_matrix.shape[1]
    n_owner = holder_assignment.shape[0]
    capacity = 3 * tok_rows // (2 * n_owner)
    own_counts = counts[0]
    upper = jnp.cumsum(own_counts)
    lower = upper - own_counts
    owner_iota = jnp.arange(n_owner, dtype=jnp.int32)
    select = holder_assignment[None, :] == owner_iota[:, None]
    owner_start = jnp.sum(jnp.where(select, lower[None, :], 0), axis=1)
    owner_count = jnp.sum(jnp.where(select, own_counts[None, :], 0), axis=1)
    slot_iota = jnp.arange(capacity, dtype=jnp.int32)
    live = slot_iota[None, :] < owner_count[:, None]
    send_index = jnp.where(live, owner_start[:, None] + slot_iota[None, :], 0).reshape(-1)
    keep = live.reshape(-1)[:, None]
    send_tokens = jnp.where(keep, jnp.take(tokens, send_index, axis=0), jnp.zeros((), tokens.dtype))
    send_cotan = jnp.where(
        keep, jnp.take(cotangent, send_index, axis=0), jnp.zeros((), cotangent.dtype)
    )
    send_tokens = send_tokens.reshape(n_owner, capacity, feat_width)
    send_cotan = send_cotan.reshape(n_owner, capacity, key_width)
    recv_tokens, recv_cotan = (
        lax.all_to_all(send_tokens, "dp", split_axis=0, concat_axis=0, tiled=True),
        lax.all_to_all(send_cotan, "dp", split_axis=0, concat_axis=0, tiled=True),
    )
    x_rows = recv_tokens.reshape(-1, feat_width)
    gradient_rows = recv_cotan.reshape(-1, key_width)
    down_half16 = adapter_down_matrix[0].astype(jnp.bfloat16)
    up_half16 = adapter_up_matrix[0].astype(jnp.bfloat16)
    hidden_part = jnp.dot(x_rows, down_half16.T, preferred_element_type=jnp.float32)
    backward_piece = adapter_scale * jnp.dot(
        gradient_rows, up_half16.T, preferred_element_type=jnp.float32
    )
    summed = lax.psum(jnp.concatenate([hidden_part, backward_piece], axis=1), "tensor")
    hidden_half16 = summed[:, :adapter_rank_width].astype(jnp.bfloat16)
    back16 = summed[:, adapter_rank_width:].astype(jnp.bfloat16)
    adapter_output = (
        adapter_scale * jnp.dot(hidden_half16, up_half16, preferred_element_type=jnp.float32)
    ).astype(jnp.bfloat16)
    adapter_grad = jnp.dot(back16, down_half16, preferred_element_type=jnp.float32).astype(
        jnp.bfloat16
    )
    down_gradient = jnp.dot(back16.T, x_rows, preferred_element_type=jnp.float32)
    up_gradient = adapter_scale * jnp.dot(
        hidden_half16.T, gradient_rows, preferred_element_type=jnp.float32
    )
    back_out, back_grad = (
        lax.all_to_all(
            adapter_output.reshape(n_owner, capacity, key_width),
            "dp",
            split_axis=0,
            concat_axis=0,
            tiled=True,
        ),
        lax.all_to_all(
            adapter_grad.reshape(n_owner, capacity, feat_width),
            "dp",
            split_axis=0,
            concat_axis=0,
            tiled=True,
        ),
    )
    base_out = jnp.dot(
        lax.all_gather(tokens, "tensor", axis=1, tiled=True),
        frozen_key_weight,
        preferred_element_type=jnp.float32,
    )
    grad_terms = jnp.dot(cotangent, frozen_key_weight.T, preferred_element_type=jnp.float32)
    base_grad = lax.psum_scatter(grad_terms, "tensor", scatter_dimension=1, tiled=True)
    token_iota = jnp.arange(tok_rows, dtype=jnp.int32)
    member = (token_iota[:, None] >= lower[None, :]) & (token_iota[:, None] < upper[None, :])
    token_owner = jnp.sum(jnp.where(member, holder_assignment[None, :], 0), axis=1)
    token_start = jnp.sum(jnp.where(member, lower[None, :], 0), axis=1)
    slot_index = token_owner * capacity + token_iota - token_start
    token_extra = jnp.take(back_out.reshape(-1, key_width), slot_index, axis=0)
    token_extra_grad = jnp.take(back_grad.reshape(-1, feat_width), slot_index, axis=0)
    layer_out = (base_out + token_extra.astype(jnp.float32)).astype(jnp.bfloat16)
    input_grad = (base_grad + token_extra_grad.astype(jnp.float32)).astype(jnp.bfloat16)
    fresh_down_matrix, fresh_down_first, fresh_down_second = optimizer_update(
        adapter_down_matrix[0], down_first_moment[0], down_second_moment[0], down_gradient
    )
    fresh_up_matrix, fresh_up_first, fresh_up_second = optimizer_update(
        adapter_up_matrix[0], up_first_moment[0], up_second_moment[0], up_gradient
    )
    return (
        layer_out,
        input_grad,
        fresh_down_matrix[None],
        fresh_down_first[None],
        fresh_down_second[None],
        fresh_up_matrix[None],
        fresh_up_first[None],
        fresh_up_second[None],
    )


def solution(mesh):
    placed = (
        P("dp", "tensor"),
        P("dp", "tensor"),
        P(None, "tensor"),
        P("dp", None),
        P(),
        P("dp", None, "tensor"),
        P("dp", None, "tensor"),
        P("dp", None, "tensor"),
        P("dp", None, "tensor"),
        P("dp", None, "tensor"),
        P("dp", None, "tensor"),
    )
    return jax.shard_map(
        per_device,
        mesh=mesh,
        in_specs=placed,
        out_specs=(
            P("dp", "tensor"),
            P("dp", "tensor"),
            P("dp", None, "tensor"),
            P("dp", None, "tensor"),
            P("dp", None, "tensor"),
            P("dp", None, "tensor"),
            P("dp", None, "tensor"),
            P("dp", None, "tensor"),
        ),
        check_vma=False,
    )
```

profile of v0, /device:TPU:11, one launch (start us, length us, event | category | flops | bytes accessed | tf_op | source)
XLA Modules:
  0.0 423.4 jit_solution(17672152602528440078)
XLA Ops:
  7.2 0.7 all-gather.2.cloned.1.call-update
  8.0 0.3 copy-done
  8.2 12.7 %fusion.32 = f32[512,8192]{1,0:T(8,128)} fusion(bf16[512,512]{1,0:T(8,128)(2,1)S(1)} %copy-done, bf16[8192,512]{1,0:T(8,128)(2,1)} %param.13), kind=kOutput, calls=%fused_computation.63 | convolution fusion | flops 4294967296 | bytes 25690112 | tf_op jit(solution)/shard_map/dot_general | solution.py:107
  20.9 0.6 copy-done.6
  21.6 0.1 copy.21
  21.7 0.1 reduce
  21.8 0.1 select_reduce_fusion.3
  22.0 0.1 select_n.104
  22.2 2.7 gather_fusion.1
  24.8 0.1 iota_compare_fusion.3
  24.9 1.2 select_select_fusion.1
  26.1 6.9 %all-to-all-start.1 = ((bf16[16,48,512]{2,1,0:T(8,128)(2,1)}), bf16[16,48,512]{2,1,0:T(8,128)(2,1)S(1)}, u32[]{:S(2)}, u32[]{:S(2)}) async-start(bf16[16,48,512]{2,1,0:T(8,128)(2,1)} %select_select_fusion.1), calls=%async_computation.1 | async-start | bytes 1572864 | tf_op jit(solution)/shard_map/all_to_all | solution.py:63
  33.0 14.7 %gather_fusion = bf16[768,4096]{1,0:T(8,128)(2,1)} fusion(bf16[512,4096]{1,0:T(8,128)(2,1)} %param.11, s32[1024]{0:T(1024)S(1)} %pad_clamp_fusion.1), kind=kCustom, calls=%fused_computation | custom fusion | bytes 12585984 | tf_op jit(solution)/shard_map/jit(_take)/gather | solution.py:55
  47.6 6.9 %select_select_fusion = bf16[16,48,4096]{2,1,0:T(8,128)(2,1)} fusion(bf16[16,48,4096]{2,1,0:T(8,128)(2,1)} %bitcast.101, pred[16,48]{1,0:T(8,128)(4,1)S(1)} %get-tuple-element.19, pred[16,48]{1,0:T(8,128)(4,1)S(1)} %get-tuple-element.18), kind=kLoop, calls=%fused_computation.6 | loop fusion | flops 6291456 | bytes 12584448 | tf_op jit(solution)/shard_map/jit(_where)/select_n | solution.py:55
  54.5 6.2 %all-to-all-start = ((bf16[16,48,4096]{2,1,0:T(8,128)(2,1)}), bf16[16,48,4096]{2,1,0:T(8,128)(2,1)}, u32[]{:S(2)}, u32[]{:S(2)}) async-start(bf16[16,48,4096]{2,1,0:T(8,128)(2,1)} %select_select_fusion), calls=%async_computation | async-start | bytes 12582912 | tf_op jit(solution)/shard_map/all_to_all | solution.py:62
  60.7 0.4 convolution_multiply_fusion
  61.1 137.3 %all-to-all-done = bf16[16,48,4096]{2,1,0:T(8,128)(2,1)} async-done(((bf16[16,48,4096]{2,1,0:T(8,128)(2,1)}), bf16[16,48,4096]{2,1,0:T(8,128)(2,1)}, u32[]{:S(2)}, u32[]{:S(2)}) %all-to-all-start) | async-done | bytes 6291488 | tf_op jit(solution)/shard_map/all_to_all | solution.py:62
  198.4 5.1 %fusion.3 = f32[768,64]{0,1:T(8,128)S(1)} fusion(bf16[768,4096]{1,0:T(8,128)(2,1)} %bitcast.4, f32[1,64,4096]{2,1,0:T(8,128)S(1)} %copy-done.2), kind=kOutput, calls=%fused_computation.18 | convolution fusion | flops 402915328 | bytes 7536640 | tf_op jit(solution)/shard_map/dot_general | solution.py:69
  203.5 23.5 %all-reduce.1 = bf16[768,128]{0,1:T(8,128)(2,1)S(1)} all-reduce(f32[768,128]{0,1:T(8,128)S(1)} %pad_maximum_fusion), channel_id=1, replica_groups=mesh['dp'=16,'tensor'=2] {'tensor'}, use_global_device_ids=true, to_apply=%region_5.6 | all-reduce | flops 98304 | bytes 589824 | tf_op jit(solution)/shard_map/psum | solution.py:73
  227.0 1.3 multiply_convert_fusion
  228.3 6.0 %all-to-all-start.2 = ((bf16[16,48,512]{2,1,0:T(8,128)(2,1)}), bf16[16,48,512]{2,1,0:T(8,128)(2,1)S(1)}, u32[]{:S(2)}, u32[]{:S(2)}) async-start(bf16[16,48,512]{2,1,0:T(8,128)(2,1)} %bitcast.105), calls=%async_computation.2 | async-start | bytes 1572864 | tf_op jit(solution)/shard_map/all_to_all | solution.py:87
  234.2 4.4 %convolution_convert_fusion = bf16[768,4096]{1,0:T(8,128)(2,1)} fusion(bf16[768,128]{0,1:T(8,128)(2,1)S(1)} %all-reduce.1, f32[1,64,4096]{2,1,0:T(8,128)S(1)} %copy-done.2), kind=kOutput, calls=%fused_computation.5 | convolution fusion | flops 402653184 | bytes 7438336 | tf_op jit(solution)/shard_map/dot_general | solution.py:79
  238.6 15.2 %all-to-all-done.2 = bf16[16,48,512]{2,1,0:T(8,128)(2,1)S(1)} async-done(((bf16[16,48,512]{2,1,0:T(8,128)(2,1)}), bf16[16,48,512]{2,1,0:T(8,128)(2,1)S(1)}, u32[]{:S(2)}, u32[]{:S(2)}) %all-to-all-start.2) | async-done | bytes 786464 | tf_op jit(solution)/shard_map/all_to_all | solution.py:87
  253.9 4.9 %all-to-all-start.3 = ((bf16[16,48,4096]{2,1,0:T(8,128)(2,1)}), bf16[16,48,4096]{2,1,0:T(8,128)(2,1)}, u32[]{:S(2)}, u32[]{:S(2)}) async-start(bf16[16,48,4096]{2,1,0:T(8,128)(2,1)} %bitcast.99), calls=%async_computation.4 | async-start | bytes 12582912 | tf_op jit(solution)/shard_map/all_to_all | solution.py:94
  258.7 0.1 select_reduce_fusion.1
  258.9 1.1 fusion.19
  260.0 6.8 %fusion.7 = (f32[1,64,4096]{2,1,0:T(8,128)}, f32[1,64,4096]{2,1,0:T(8,128)}, f32[1,64,4096]{2,1,0:T(8,128)}) fusion(f32[1,64,4096]{2,1,0:T(8,128)} %param.19, f32[1,64,4096]{2,1,0:T(8,128)} %param.18, f32[1,64,4096]{2,1,0:T(8,128)S(1)} %copy-done.2, bf16[768,4096]{1,0:T(8,128)(2,1)} %bitcast.4, bf16[768,128]{0,1:T(8,128)(2,1)S(1)} %all-reduce.1), kind=kOutput, calls=%fused_computation.23 | convolution fusion | flops 405798912 | bytes 12681216 | tf_op jit(solution)/shard_map/dot_general | solution.py:82
  266.8 2.0 gather_fusion.2
  268.8 11.3 %fusion = bf16[512,512]{1,0:T(8,128)(2,1)} fusion(bf16[512,8192]{1,0:T(8,128)(2,1)} %all-gather.2.cloned.1.call-done, bf16[8192,512]{1,0:T(8,128)(2,1)} %param.13, bf16[512,512]{1,0:T(8,128)(2,1)S(1)} %gather_fusion.2, pred[512]{0:T(512)(128)(4,1)S(1)} %compare_and_fusion.1), kind=kOutput, calls=%fused_computation.10 | convolution fusion | flops 4296015872 | bytes 17826304 | tf_op jit(solution)/shard_map/dot_general | solution.py:102
  280.1 115.9 %all-to-all-done.3 = bf16[16,48,4096]{2,1,0:T(8,128)(2,1)} async-done(((bf16[16,48,4096]{2,1,0:T(8,128)(2,1)}), bf16[16,48,4096]{2,1,0:T(8,128)(2,1)}, u32[]{:S(2)}, u32[]{:S(2)}) %all-to-all-start.3) | async-done | bytes 6291488 | tf_op jit(solution)/shard_map/all_to_all | solution.py:94
  396.0 12.2 %gather_fusion.3 = bf16[512,4096]{1,0:T(8,128)(2,1)} fusion(bf16[768,4096]{1,0:T(8,128)(2,1)} %bitcast.17, s32[1024]{0:T(1024)S(1)} %pad_clamp_fusion), kind=kCustom, calls=%fused_computation.3 | custom fusion | bytes 8390656 | tf_op jit(solution)/shard_map/jit(_take)/gather | solution.py:115
  408.2 8.4 %add_convert_fusion = bf16[512,4096]{1,0:T(8,128)(2,1)} fusion(f32[512,4096]{1,0:T(8,128)} %reduce-scatter.2.cloned.1.call-done, bf16[512,4096]{1,0:T(8,128)(2,1)} %gather_fusion.3, pred[512]{0:T(512)(128)(4,1)S(1)} %compare_and_fusion.1), kind=kLoop, calls=%fused_computation.4 | loop fusion | flops 8388608 | bytes 16777728 | tf_op jit(solution)/shard_map/convert_element_type | solution.py:117
  (30 shorter events, 0.4 us)
Async XLA Ops:
  7.2 1.1 copy-start
  7.2 261.6 %all-gather.2.cloned.1.call-start = ((), (), s32[]{:S(2)}) async-start(), calls=%async_computation.5 | async-start | bytes 12582912 | tf_op jit(solution)/shard_map/all_gather | solution.py:103
  7.9 400.3 %reduce-scatter.2.cloned.1.call-start = ((), (), s32[]{:S(2)}) async-start(), calls=%async_computation.6 | async-start | bytes 25165824 | tf_op jit(solution)/shard_map/reduce_scatter | solution.py:108
  20.9 0.7 copy-start.6
  20.9 0.9 copy-start.7
  26.1 28.4 %all-to-all-start.1 = ((bf16[16,48,512]{2,1,0:T(8,128)(2,1)}), bf16[16,48,512]{2,1,0:T(8,128)(2,1)S(1)}, u32[]{:S(2)}, u32[]{:S(2)}) async-start(bf16[16,48,512]{2,1,0:T(8,128)(2,1)} %select_select_fusion.1), calls=%async_computation.1 | async-start | bytes 1572864 | tf_op jit(solution)/shard_map/all_to_all | solution.py:63
  54.5 6.2 %copy-start.3 = (f32[1,64,512]{2,1,0:T(8,128)S(1)}, f32[1,64,512]{2,1,0:T(8,128)}, u32[]{:S(2)}) copy-start(f32[1,64,512]{2,1,0:T(8,128)} %param.17) | copy-start | bytes 393220
  54.5 143.9 %copy-start.2 = (f32[1,64,4096]{2,1,0:T(8,128)S(1)}, f32[1,64,4096]{2,1,0:T(8,128)}, u32[]{:S(2)}) copy-start(f32[1,64,4096]{2,1,0:T(8,128)} %param.16) | copy-start | bytes 3145732
  54.5 143.9 %all-to-all-start = ((bf16[16,48,4096]{2,1,0:T(8,128)(2,1)}), bf16[16,48,4096]{2,1,0:T(8,128)(2,1)}, u32[]{:S(2)}, u32[]{:S(2)}) async-start(bf16[16,48,4096]{2,1,0:T(8,128)(2,1)} %select_select_fusion), calls=%async_computation | async-start | bytes 12582912 | tf_op jit(solution)/shard_map/all_to_all | solution.py:62
  228.3 25.6 %all-to-all-start.2 = ((bf16[16,48,512]{2,1,0:T(8,128)(2,1)}), bf16[16,48,512]{2,1,0:T(8,128)(2,1)S(1)}, u32[]{:S(2)}, u32[]{:S(2)}) async-start(bf16[16,48,512]{2,1,0:T(8,128)(2,1)} %bitcast.105), calls=%async_computation.2 | async-start | bytes 1572864 | tf_op jit(solution)/shard_map/all_to_all | solution.py:87
  253.9 5.0 %copy-start.4 = (f32[1,64,512]{2,1,0:T(8,128)S(1)}, f32[1,64,512]{2,1,0:T(8,128)}, u32[]{:S(2)}) copy-start(f32[1,64,512]{2,1,0:T(8,128)} %param.21) | copy-start | bytes 393220
  253.9 5.0 %copy-start.5 = (f32[1,64,512]{2,1,0:T(8,128)S(1)}, f32[1,64,512]{2,1,0:T(8,128)}, u32[]{:S(2)}) copy-start(f32[1,64,512]{2,1,0:T(8,128)} %param.20) | copy-start | bytes 393220
  253.9 142.1 %all-to-all-start.3 = ((bf16[16,48,4096]{2,1,0:T(8,128)(2,1)}), bf16[16,48,4096]{2,1,0:T(8,128)(2,1)}, u32[]{:S(2)}, u32[]{:S(2)}) async-start(bf16[16,48,4096]{2,1,0:T(8,128)(2,1)} %bitcast.99), calls=%async_computation.4 | async-start | bytes 12582912 | tf_op jit(solution)/shard_map/all_to_all | solution.py:94
  396.0 20.6 %copy-start.1 = (bf16[512,512]{1,0:T(8,128)(2,1)S(1)}, bf16[512,512]{1,0:T(8,128)(2,1)}, u32[]{:S(2)}) copy-start(bf16[512,512]{1,0:T(8,128)(2,1)} %param.12) | copy-start | bytes 1572868
Sparse Core Ops, SparseCore 0:
  9.6 105.1 all-gather.1
  117.0 197.5 reduce-scatter.1
where the time goes:
time: 424 us; the launch traced here: 423 us
  waiting for transfers between devices  269 us (63%)
  matrix products  43 us (10%)
  local copies, waits for them, and re-layouts  32.6 us (8%)
  starting transfers between devices  23.9 us (6%)
  blocking collectives  23.5 us (6%)
  other arithmetic  17.1 us (4%)
  between operations  14.2 us (3%)
    all_to_all x1, waiting for transfers between devices, per_device(): lax.all_to_all(send_tokens, 'dp', split_axis=0, concat_axis=0, tiled=True)  137 us
    all_to_all x1, waiting for transfers between devices, per_device(): lax.all_to_all(adapter_grad.reshape(n_owner, capacity, feat_width), 'dp',...  116 us
    psum x1, blocking collectives, per_device(): lax.psum(jnp.concatenate([hidden_part, backward_piece], axis=1), 'tensor')  23.5 us
    all_to_all x1, waiting for transfers between devices, per_device(): lax.all_to_all(adapter_output.reshape(n_owner, capacity, key_width), 'dp'...  15.2 us
    gather x1, local copies, waits for them, and re-layouts, per_device(): jnp.take(tokens, send_index, axis=0)  14.7 us
    dot_general x1, matrix products, per_device(): jnp.dot(cotangent, frozen_key_weight.T, preferred_element_type=jnp.float32)  12.7 us
    gather x1, local copies, waits for them, and re-layouts, per_device(): jnp.take(back_grad.reshape(-1, feat_width), slot_index, axis=0)  12.2 us
    dot_general x1, matrix products, per_device(): jnp.dot(lax.all_gather(tokens, 'tensor', axis=1, tiled=True), frozen_key_...  11.3 us
  transfers between devices with their start and end apart: 6, of which 3 were waited for; matrix products, arithmetic and copies ran while one was open for 20% of the time, Pallas kernels for 0%

commit v1 on v0

v1 whole, which is shorter than its diff:
```python
import jax
import jax.numpy as jnp
from jax import lax
from jax.sharding import PartitionSpec as P

adapter_scale = 2.0
learn_rate = 0.01
beta_one = 0.9
beta_two = 0.999
adam_eps = 1e-08
adam_step = 10


def optimizer_update(weight, moment, second, grad):
    moment_new = beta_one * moment + (1.0 - beta_one) * grad
    second_new = beta_two * second + (1.0 - beta_two) * grad * grad
    first_fix = 1.0 - beta_one**adam_step
    second_fix = 1.0 - beta_two**adam_step
    weight_new = weight - learn_rate * (moment_new / first_fix) / (
        jnp.sqrt(second_new / second_fix) + adam_eps
    )
    return (weight_new, moment_new, second_new)


def owner_mask(counts_row, holders, rows, rank):
    n_owner = holders.shape[0]
    order = jnp.arange(n_owner, dtype=jnp.int32)
    upper = jnp.sum(jnp.where(order[None, :] <= order[:, None], counts_row[None, :], 0), axis=1)
    lower = upper - counts_row
    select = holders[None, :] == jnp.arange(n_owner, dtype=jnp.int32)[:, None]
    start = jnp.sum(jnp.where(select, lower[None, :], 0), axis=1)
    stop = jnp.sum(jnp.where(select, upper[None, :], 0), axis=1)
    start = jnp.repeat(start, rank)
    stop = jnp.repeat(stop, rank)
    token = jnp.arange(rows, dtype=jnp.int32)[:, None]
    return (token >= start[None, :]) & (token < stop[None, :])


def fold(masked, width):
    total = masked[:, :width]
    for k in range(1, masked.shape[1] // width):
        total = total + masked[:, k * width : (k + 1) * width]
    return total


def dot(a, b, contract):
    return lax.dot_general(a, b, (contract, ((), ())), preferred_element_type=jnp.float32)


def make(n_dp, n_tensor):
    def ring(shift):
        return [(i, (i + shift) % n_tensor) for i in range(n_tensor)]

    swap_core = [(i, i ^ 1) for i in range(n_dp)]

    def per_device(
        tokens,
        cotangent,
        frozen_key_weight,
        counts,
        holder_assignment,
        adapter_down_matrix,
        adapter_up_matrix,
        down_first_moment,
        down_second_moment,
        up_first_moment,
        up_second_moment,
    ):
        rows, feat = tokens.shape
        keys = cotangent.shape[1]
        rank = adapter_down_matrix.shape[1]
        n_owner = holder_assignment.shape[0]
        width = 2 * rank
        half = feat // 2
        mine = lax.axis_index("tensor")
        core = lax.axis_index("dp") % 2
        bf = jnp.bfloat16

        both16 = jnp.concatenate(
            [adapter_down_matrix[0].astype(bf), adapter_up_matrix[0].astype(bf)], axis=1
        )
        all16 = lax.all_gather(both16, "dp", axis=0, tiled=True)

        weight_mine = lax.dynamic_slice_in_dim(frozen_key_weight, mine * feat, feat, 0)
        cots, weights = [cotangent], [weight_mine]
        for shift in range(1, n_tensor):
            cots.append(lax.ppermute(cotangent, "tensor", ring(shift)))
            target = lax.rem(mine + shift, n_tensor)
            got = lax.ppermute(
                lax.dynamic_slice_in_dim(frozen_key_weight, target * feat + core * half, half, 0),
                "tensor",
                ring(shift),
            )
            got_peer = lax.ppermute(got, "dp", swap_core)
            weights.append(
                jnp.concatenate(
                    [jnp.where(core == 0, got, got_peer), jnp.where(core == 0, got_peer, got)],
                    axis=0,
                )
            )

        base_out = dot(tokens, weight_mine, ((1,), (0,)))
        for shift in range(1, n_tensor):
            base_out = base_out + lax.ppermute(
                dot(tokens, weights[shift], ((1,), (0,))), "tensor", ring(-shift)
            )

        mask = owner_mask(counts[0], holder_assignment, rows, rank)
        down_all = all16[:, :feat]
        up_all = all16[:, feat:]
        hidden_part = fold(jnp.where(mask, dot(tokens, down_all, ((1,), (1,))), 0.0), width)
        back_part = fold(jnp.where(mask, dot(cotangent, up_all, ((1,), (1,))), 0.0), width)
        part = jnp.concatenate([hidden_part, adapter_scale * back_part], axis=1)
        summed = part
        for shift in range(1, n_tensor):
            summed = summed + lax.ppermute(part, "tensor", ring(shift))
        times = n_owner * rank // width
        zero = jnp.zeros((), bf)
        hidden16 = jnp.where(mask, jnp.tile(summed[:, :width].astype(bf), (1, times)), zero)
        back16 = jnp.where(mask, jnp.tile(summed[:, width:].astype(bf), (1, times)), zero)

        down_part = dot(back16, tokens, ((0,), (0,)))
        up_part = adapter_scale * dot(hidden16, cotangent, ((0,), (0,)))
        down_gradient = lax.psum_scatter(down_part, "dp", scatter_dimension=0, tiled=True)
        up_gradient = lax.psum_scatter(up_part, "dp", scatter_dimension=0, tiled=True)

        layer_out = (
            base_out + adapter_scale * dot(hidden16, up_all, ((1,), (0,)))
        ).astype(bf)
        base_grad = dot(back16, down_all, ((1,), (0,)))
        for cot, weight in zip(cots, weights):
            base_grad = base_grad + dot(cot, weight, ((1,), (1,)))
        input_grad = base_grad.astype(bf)
        fresh_down = optimizer_update(
            adapter_down_matrix[0], down_first_moment[0], down_second_moment[0], down_gradient
        )
        fresh_up = optimizer_update(
            adapter_up_matrix[0], up_first_moment[0], up_second_moment[0], up_gradient
        )
        return (layer_out, input_grad) + tuple(x[None] for x in fresh_down + fresh_up)

    return per_device


def solution(mesh):
    placed = (
        P("dp", "tensor"),
        P("dp", "tensor"),
        P(None, "tensor"),
        P("dp", None),
        P(),
        P("dp", None, "tensor"),
        P("dp", None, "tensor"),
        P("dp", None, "tensor"),
        P("dp", None, "tensor"),
        P("dp", None, "tensor"),
        P("dp", None, "tensor"),
    )
    return jax.shard_map(
        make(mesh.shape["dp"], mesh.shape["tensor"]),
        mesh=mesh,
        in_specs=placed,
        out_specs=(
            P("dp", "tensor"),
            P("dp", "tensor"),
            P("dp", None, "tensor"),
            P("dp", None, "tensor"),
            P("dp", None, "tensor"),
            P("dp", None, "tensor"),
            P("dp", None, "tensor"),
            P("dp", None, "tensor"),
        ),
        check_vma=False,
    )
```

time: 424 us -> 378 us (0.89)
  local copies, waits for them, and re-layouts: 32.6 us -> 6.24 us
  blocking collectives: 23.5 us -> 0 us
  starting transfers between devices: 23.9 us -> 6.08 us
  matrix products: 43 us -> 58.3 us
  waiting for transfers between devices: 269 us -> 274 us
    all_to_all x4 -> x0, waiting for transfers between devices: 268 us -> none  [the longest x1 137 us: per_device(): lax.all_to_all(send_tokens, 'dp', split_axis=0, concat_axis=0, tiled=True)]
    reduce_scatter x1 -> x2, waiting for transfers between devices: 0.01 us -> 123 us  [the longest x1 123 us: per_device(): lax.psum_scatter(down_part, 'dp', scatter_dimension=0, tiled=True)]
    all_gather x1, waiting for transfers between devices: 0.02 us -> 79.3 us  [per_device(): all16 = lax.all_gather(both16, 'dp', axis=0, tiled=True)]
    ppermute x0 -> x5, waiting for transfers between devices: none -> 71.5 us  [the longest x1 44.9 us: per_device(): lax.ppermute(lax.dynamic_slice_in_dim(frozen_key_weight, target * feat +...]
    gather x4 -> x0, local copies, waits for them, and re-layouts: 31.5 us -> none  [the longest x1 14.7 us: per_device(): jnp.take(tokens, send_index, axis=0)]
    all_to_all x4 -> x0, starting transfers between devices: 23.9 us -> none  [the longest x1 6.89 us: per_device(): lax.all_to_all(send_cotan, 'dp', split_axis=0, concat_axis=0, tiled=True)]
    psum x1 -> x0, blocking collectives: 23.5 us -> none  [per_device(): lax.psum(jnp.concatenate([hidden_part, backward_piece], axis=1), 'tensor')]
    dot_general x8 -> x10, matrix products: 43 us -> 58.3 us  [dot(): lax.dot_general(a, b, (contract, ((), ())), preferred_element_type=jnp.fl...]
  transfers between devices with their start and end apart: 6 -> 8, of which waited for: 3 -> 5; matrix products, arithmetic and copies ran while one was open for 20% -> 15% of each run, Pallas kernels for 0% -> 0%
where the time goes in v1:
time: 378 us; the launch traced here: 375 us
  waiting for transfers between devices  274 us (72%)
  matrix products  58.3 us (15%)
  other arithmetic  16.4 us (4%)
  between operations  14 us (4%)
  local copies, waits for them, and re-layouts  6.24 us (2%)
  starting transfers between devices  6.08 us (2%)
    reduce_scatter x1, waiting for transfers between devices, per_device(): lax.psum_scatter(down_part, 'dp', scatter_dimension=0, tiled=True)  123 us
    all_gather x1, waiting for transfers between devices, per_device(): all16 = lax.all_gather(both16, 'dp', axis=0, tiled=True)  79.3 us
    dot_general x10, matrix products, dot(): lax.dot_general(a, b, (contract, ((), ())), preferred_element_type=jnp.fl...  58.3 us
    ppermute x1, waiting for transfers between devices, per_device(): lax.ppermute(lax.dynamic_slice_in_dim(frozen_key_weight, target * feat +...  44.9 us
    ppermute x1, waiting for transfers between devices, per_device(): lax.ppermute(dot(tokens, weights[shift], ((1,), (0,))), 'tensor', ring(-s...  14.5 us
    ppermute x1, waiting for transfers between devices, per_device(): summed = summed + lax.ppermute(part, 'tensor', ring(shift))  12.1 us
  transfers between devices with their start and end apart: 8, of which 5 were waited for; matrix products, arithmetic and copies ran while one was open for 15% of the time, Pallas kernels for 0%

profile of v1, /device:TPU:11, one launch (start us, length us, event | category | flops | bytes accessed | tf_op | source)
XLA Modules:
  0.0 374.6 jit_solution(975520279979545235)
XLA Ops:
  7.2 0.9 bitcast_convert_fusion.1
  8.1 1.3 bitcast_convert_fusion
  9.4 0.9 pad_maximum_fusion.5
  10.3 0.8 select_reduce_fusion.2
  11.8 0.8 select_reduce_fusion.1
  12.8 79.3 %all-gather.2.cloned.1.call-done = bf16[1024,4608]{1,0:T(8,128)(2,1)} async-done(((bf16[64,4608]{1,0:T(8,128)(2,1)}), bf16[1024,4608]{1,0:T(8,128)(2,1)}) %all-gather.2.cloned.1.call-update) | async-done | bytes 9437200 | tf_op jit(solution)/shard_map/all_gather | solution.py:82
  92.2 2.5 bitcast_select_fusion
  94.9 7.5 %bitcast_select_fusion.1 = f32[512,1024]{0,1:T(8,128)S(1)} fusion(bf16[512,4096]{1,0:T(8,128)(2,1)S(1)} %copy-done.8, bf16[1024,4608]{1,0:T(8,128)(2,1)} %all-gather.2.cloned.1.call-done, s32[1024]{0:T(1024)S(1)} %lt.28, s32[1024]{0:T(1024)S(1)} %ge.18), kind=kOutput, calls=%fused_computation.14 | convolution fusion | flops 4297064448 | bytes 14688256 | tf_op jit(solution)/shard_map/dot_general | solution.py:47
  102.7 1.3 collective-permute-start.3
  104.0 12.1 %collective-permute-done.3 = f32[512,256]{0,1:T(8,128)S(1)} collective-permute-done((f32[512,256]{0,1:T(8,128)S(1)}, f32[512,256]{0,1:T(8,128)S(1)}, u32[]{:S(2)}, u32[]{:S(2)}) %collective-permute-start.3) | collective-permute-done | bytes 524320 | tf_op jit(solution)/shard_map/ppermute | solution.py:116
  116.2 0.9 bitcast_select_fusion.2
  117.1 1.0 copy-done.2
  118.0 3.0 convolution_multiply_fusion
  121.3 10.5 %fusion.34 = f32[1024,4096]{1,0:T(8,128)} fusion(bf16[512,1024]{0,1:T(8,128)(2,1)S(1)} %get-tuple-element.36, bf16[512,4096]{1,0:T(8,128)(2,1)} %param.11), kind=kOutput, calls=%fused_computation.76 | convolution fusion | flops 4294967296 | bytes 22020096 | tf_op jit(solution)/shard_map/dot_general | solution.py:47
  131.9 1.8 constant_dynamic-slice_fusion
  133.7 1.3 collective-permute-start
  135.0 44.9 %collective-permute-done = bf16[2048,512]{1,0:T(8,128)(2,1)S(1)} collective-permute-done((bf16[2048,512]{1,0:T(8,128)(2,1)S(1)}, bf16[2048,512]{1,0:T(8,128)(2,1)S(1)}, u32[]{:S(2)}, u32[]{:S(2)}) %collective-permute-start) | collective-permute-done | bytes 2097184 | tf_op jit(solution)/shard_map/ppermute | solution.py:89
  179.9 2.0 collective-permute-start.1
  181.8 1.2 collective-permute-start.4
  183.0 8.1 %fusion.5 = f32[4096,512]{0,1:T(8,128)} fusion(bf16[512,512]{1,0:T(8,128)(2,1)} %param.12, bf16[8192,512]{1,0:T(8,128)(2,1)} %param.13, s32[]{:T(128)S(6)} %select_n.49), kind=kOutput, calls=%fused_computation.8 | convolution fusion | flops 2147483648 | bytes 13107204 | tf_op jit(solution)/shard_map/dot_general | solution.py:47
  191.1 5.0 %fusion.14 = f32[512,512]{0,1:T(8,128)S(1)} fusion(bf16[512,4096]{1,0:T(8,128)(2,1)S(1)} %copy-done.9, bf16[8192,512]{1,0:T(8,128)(2,1)} %param.13, s32[]{:T(128)S(6)} %select_n.49), kind=kOutput, calls=%fused_computation.23 | convolution fusion | flops 2147483648 | bytes 9437188 | tf_op jit(solution)/shard_map/dot_general | solution.py:47
  196.2 3.5 broadcast_select_fusion.1
  199.7 2.4 fusion.13
  202.2 1.8 slice-done.1
  204.3 7.2 %fusion.1 = f32[512,4096]{1,0:T(8,128)} fusion(bf16[512,1024]{0,1:T(8,128)(2,1)S(1)} %get-tuple-element.36, bf16[1024,4608]{1,0:T(8,128)(2,1)S(1)} %bitcast.86), kind=kOutput, calls=%fused_computation.3 | convolution fusion | flops 4294967296 | bytes 17825792 | tf_op jit(solution)/shard_map/dot_general | solution.py:47
  211.5 0.8 convolution_multiply_fusion.1
  212.2 14.5 %collective-permute-done.2 = f32[512,512]{0,1:T(8,128)S(1)} collective-permute-done((f32[512,512]{0,1:T(8,128)S(1)}, f32[512,512]{0,1:T(8,128)S(1)}, u32[]{:S(2)}, u32[]{:S(2)}) %collective-permute-start.2) | collective-permute-done | bytes 1048608 | tf_op jit(solution)/shard_map/ppermute | solution.py:104
  227.2 1.0 copy.26
  228.2 11.2 %fusion = bf16[512,4096]{1,0:T(8,128)(2,1)} fusion(f32[512,4096]{1,0:T(8,128)} %fusion.1, f32[4096,512]{0,1:T(8,128)} %fusion.5, bf16[512,512]{1,0:T(8,128)(2,1)} %collective-permute-done.4, bf16[2048,512]{1,0:T(8,128)(2,1)} %copy-done, bf16[2048,512]{1,0:T(8,128)(2,1)S(1)} %get-tuple-element.26), kind=kOutput, calls=%fused_computation.1 | convolution fusion | flops 2162163712 | bytes 25690112 | tf_op jit(solution)/shard_map/dot_general | solution.py:47
  239.4 1.7 fusion.27
  241.1 122.8 %reduce-scatter.3.cloned.1.call-done = f32[64,4096]{1,0:T(8,128)} async-done(((f32[1024,4096]{1,0:T(8,128)}), f32[64,4096]{1,0:T(8,128)}) %reduce-scatter.3.cloned.1.call-update) | async-done | bytes 1048592 | tf_op jit(solution)/shard_map/reduce_scatter | solution.py:124
  363.9 4.2 %fusion.22 = (f32[1,64,4096]{2,1,0:T(8,128)}, f32[1,64,4096]{2,1,0:T(8,128)}, f32[1,64,4096]{2,1,0:T(8,128)}) fusion(f32[64,4096]{1,0:T(8,128)} %reduce-scatter.3.cloned.1.call-done, f32[1,64,4096]{2,1,0:T(8,128)} %param.19, f32[1,64,4096]{2,1,0:T(8,128)} %param.18, f32[1,64,4096]{2,1,0:T(8,128)S(1)} %copy-done.1), kind=kLoop, calls=%fused_computation.39 | loop fusion | flops 3145728 | bytes 7340032 | tf_op jit(solution)/shard_map/broadcast_in_dim | solution.py:140
  (46 shorter events, 2.8 us)
Async XLA Ops:
  7.2 85.0 %all-gather.2.cloned.1.call-start = ((), (), s32[]{:S(2)}) async-start(), calls=%async_computation.2 | async-start | bytes 10027008 | tf_op jit(solution)/shard_map/all_gather | solution.py:82
  10.3 229.1 %reduce-scatter.5.cloned.1.call-start = ((), (), s32[]{:S(2)}) async-start(), calls=%async_computation.4 | async-start | bytes 2228224 | tf_op jit(solution)/shard_map/reduce_scatter | solution.py:125
  92.1 2.8 copy-start.8
  102.7 13.3 %collective-permute-start.3 = (f32[512,256]{0,1:T(8,128)S(1)}, f32[512,256]{0,1:T(8,128)S(1)}, u32[]{:S(2)}, u32[]{:S(2)}) collective-permute-start(f32[512,256]{0,1:T(8,128)S(1)} %pad_maximum_fusion.6), channel_id=1, source_target_pairs={{0,1},{1,0},{2,3},{3,2},{4,5},{5,4},{6,7},{7,6},{8,9},{9,8},{10,11... | collective-permute-start | bytes 1572872 | tf_op jit(solution)/shard_map/ppermute | solution.py:116
  117.1 1.0 copy-start.2
  121.1 242.8 %reduce-scatter.3.cloned.1.call-start = ((), (), s32[]{:S(2)}) async-start(), calls=%async_computation.3 | async-start | bytes 17825792 | tf_op jit(solution)/shard_map/reduce_scatter | solution.py:124
  133.7 46.1 %collective-permute-start = (bf16[2048,512]{1,0:T(8,128)(2,1)S(1)}, bf16[2048,512]{1,0:T(8,128)(2,1)S(1)}, u32[]{:S(2)}, u32[]{:S(2)}) collective-permute-start(bf16[2048,512]{1,0:T(8,128)(2,1)S(1)} %constant_dynamic-slice_fusion), channel_id=1, source_target_pairs={{0,1},{1,0},{2,3},{3,2},{4,5},{5,4},{6,7},{7,6},{8,9},{9,8},{10,11... | collective-permute-start | bytes 6291464 | tf_op jit(solution)/shard_map/ppermute | solution.py:89
  179.9 11.3 %copy-start.4 = (bf16[2048,512]{1,0:T(8,128)(2,1)}, bf16[2048,512]{1,0:T(8,128)(2,1)S(1)}, u32[]{:S(2)}) copy-start(bf16[2048,512]{1,0:T(8,128)(2,1)S(1)} %collective-permute-done) | copy-start | bytes 6291460
  179.9 16.3 %collective-permute-start.1 = (bf16[2048,512]{1,0:T(8,128)(2,1)S(1)}, bf16[2048,512]{1,0:T(8,128)(2,1)}, u32[]{:S(2)}, u32[]{:S(2)}) collective-permute-start(bf16[2048,512]{1,0:T(8,128)(2,1)S(1)} %collective-permute-done), channel_id=1, source_target_pairs={{0,2},{2,0},{4,6},{6,4},{8,10},{10,8},{12,14},{14,12},{16,18},{18,... | collective-permute-start | bytes 6291464 | tf_op jit(solution)/shard_map/ppermute | solution.py:94
  181.8 46.3 %collective-permute-start.4 = (bf16[512,512]{1,0:T(8,128)(2,1)}, bf16[512,512]{1,0:T(8,128)(2,1)}, u32[]{:S(2)}, u32[]{:S(2)}) collective-permute-start(bf16[512,512]{1,0:T(8,128)(2,1)} %param.12), channel_id=1, source_target_pairs={{0,1},{1,0},{2,3},{3,2},{4,5},{5,4},{6,7},{7,6},{8,9},{9,8},{10,11... | collective-permute-start | bytes 1572872 | tf_op jit(solution)/shard_map/ppermute | solution.py:87
  183.0 8.1 %copy-start.9 = (bf16[512,4096]{1,0:T(8,128)(2,1)S(1)}, bf16[512,4096]{1,0:T(8,128)(2,1)}, u32[]{:S(2)}) copy-start(bf16[512,4096]{1,0:T(8,128)(2,1)} %param.11) | copy-start | bytes 12582916
  196.2 6.0 %slice-start = ((s8[9437184]{0:T(1024)(128)(4,1)}), s8[4194304]{0:T(1024)(128)(4,1)S(1)}, s32[]{:S(2)}) async-start(s8[9437184]{0:T(1024)(128)(4,1)} %bitcast.85), calls=%async_computation.5 | async-start | bytes 8388608
  196.2 7.8 %slice-start.1 = ((s8[9437184]{0:T(1024)(128)(4,1)}), s8[4194304]{0:T(1024)(128)(4,1)S(1)}, s32[]{:S(2)}) async-start(s8[9437184]{0:T(1024)(128)(4,1)} %bitcast.85), calls=%async_computation.6 | async-start | bytes 8388608
  199.6 2.4 copy-start
  199.6 4.7 %slice-start.2 = ((s8[9437184]{0:T(1024)(128)(4,1)}), s8[1048576]{0:T(1024)(128)(4,1)S(1)}, s32[]{:S(2)}) async-start(s8[9437184]{0:T(1024)(128)(4,1)} %bitcast.85), calls=%async_computation.7 | async-start | bytes 2097152
  202.1 9.4 %copy-start.3 = (bf16[512,1024]{0,1:T(8,128)(2,1)S(1)}, bf16[512,1024]{0,1:T(8,128)(2,1)}, u32[]{:S(2)}) copy-start(bf16[512,1024]{0,1:T(8,128)(2,1)} %copy-done.2) | copy-start | bytes 3145732
  202.1 24.7 %collective-permute-start.2 = (f32[512,512]{0,1:T(8,128)S(1)}, f32[512,512]{0,1:T(8,128)S(1)}, u32[]{:S(2)}, u32[]{:S(2)}) collective-permute-start(f32[512,512]{0,1:T(8,128)S(1)} %fusion.13), channel_id=1, source_target_pairs={{0,1},{1,0},{2,3},{3,2},{4,5},{5,4},{6,7},{7,6},{8,9},{9,8},{10,11... | collective-permute-start | bytes 3145736 | tf_op jit(solution)/shard_map/ppermute | solution.py:104
  228.2 11.2 %copy-start.5 = (f32[1,64,512]{2,1,0:T(8,128)S(1)}, f32[1,64,512]{2,1,0:T(8,128)}, u32[]{:S(2)}) copy-start(f32[1,64,512]{2,1,0:T(8,128)} %param.17) | copy-start | bytes 393220
  228.2 11.2 %copy-start.6 = (f32[1,64,512]{2,1,0:T(8,128)S(1)}, f32[1,64,512]{2,1,0:T(8,128)}, u32[]{:S(2)}) copy-start(f32[1,64,512]{2,1,0:T(8,128)} %param.21) | copy-start | bytes 393220
  228.2 11.2 %copy-start.7 = (f32[1,64,512]{2,1,0:T(8,128)S(1)}, f32[1,64,512]{2,1,0:T(8,128)}, u32[]{:S(2)}) copy-start(f32[1,64,512]{2,1,0:T(8,128)} %param.20) | copy-start | bytes 393220
  228.2 135.7 %copy-start.1 = (f32[1,64,4096]{2,1,0:T(8,128)S(1)}, f32[1,64,4096]{2,1,0:T(8,128)}, u32[]{:S(2)}) copy-start(f32[1,64,4096]{2,1,0:T(8,128)} %param.16) | copy-start | bytes 3145732
Sparse Core Ops, SparseCore 0:
  10.9 81.2 all-gather.1
  121.2 59.8 reduce-scatter.4
  185.8 178.0 reduce-scatter.2

commit v2 on v1

--- a/solution.py
+++ b/solution.py
@@ -22,7 +22,7 @@
     return (weight_new, moment_new, second_new)
 
 
-def owner_mask(counts_row, holders, rows, rank):
+def owner_masks(counts_row, holders, rows, rank):
     n_owner = holders.shape[0]
     order = jnp.arange(n_owner, dtype=jnp.int32)
     upper = jnp.sum(jnp.where(order[None, :] <= order[:, None], counts_row[None, :], 0), axis=1)
@@ -30,10 +30,15 @@
     select = holders[None, :] == jnp.arange(n_owner, dtype=jnp.int32)[:, None]
     start = jnp.sum(jnp.where(select, lower[None, :], 0), axis=1)
     stop = jnp.sum(jnp.where(select, upper[None, :], 0), axis=1)
+    capacity = 3 * rows // (2 * n_owner)
+    token = jnp.arange(rows, dtype=jnp.int32)
+    slot_token = (start[:, None] + jnp.arange(capacity, dtype=jnp.int32)[None, :]).reshape(-1)
+    slot_stop = jnp.repeat(stop, capacity)
+    slots = (token[None, :] == slot_token[:, None]) & (token[None, :] < slot_stop[:, None])
     start = jnp.repeat(start, rank)
     stop = jnp.repeat(stop, rank)
-    token = jnp.arange(rows, dtype=jnp.int32)[:, None]
-    return (token >= start[None, :]) & (token < stop[None, :])
+    mask = (token[:, None] >= start[None, :]) & (token[:, None] < stop[None, :])
+    return mask, slots
 
 
 def fold(masked, width):
@@ -76,6 +81,14 @@
         core = lax.axis_index("dp") % 2
         bf = jnp.bfloat16
 
+        mask, slots = owner_masks(counts[0], holder_assignment, rows, rank)
+        pick = slots.astype(bf)
+        send = jnp.concatenate(
+            [dot(pick, x, ((1,), (0,))).astype(bf) for x in (tokens, cotangent)], axis=1
+        )
+        routed = lax.all_to_all(
+            send.reshape(n_owner, -1, feat + keys), "dp", split_axis=0, concat_axis=0, tiled=True
+        ).reshape(-1, feat + keys)
         both16 = jnp.concatenate(
             [adapter_down_matrix[0].astype(bf), adapter_up_matrix[0].astype(bf)], axis=1
         )
@@ -105,7 +118,6 @@
                 dot(tokens, weights[shift], ((1,), (0,))), "tensor", ring(-shift)
             )
 
-        mask = owner_mask(counts[0], holder_assignment, rows, rank)
         down_all = all16[:, :feat]
         up_all = all16[:, feat:]
         hidden_part = fold(jnp.where(mask, dot(tokens, down_all, ((1,), (1,))), 0.0), width)
@@ -119,10 +131,20 @@
         hidden16 = jnp.where(mask, jnp.tile(summed[:, :width].astype(bf), (1, times)), zero)
         back16 = jnp.where(mask, jnp.tile(summed[:, width:].astype(bf), (1, times)), zero)
 
-        down_part = dot(back16, tokens, ((0,), (0,)))
-        up_part = adapter_scale * dot(hidden16, cotangent, ((0,), (0,)))
-        down_gradient = lax.psum_scatter(down_part, "dp", scatter_dimension=0, tiled=True)
-        up_gradient = lax.psum_scatter(up_part, "dp", scatter_dimension=0, tiled=True)
+        x_rows, cot_rows = routed[:, :feat], routed[:, feat:]
+        own_part = jnp.concatenate(
+            [
+                dot(x_rows, both16[:, :feat], ((1,), (1,))),
+                adapter_scale * dot(cot_rows, both16[:, feat:], ((1,), (1,))),
+            ],
+            axis=1,
+        )
+        own = own_part
+        for shift in range(1, n_tensor):
+            own = own + lax.ppermute(own_part, "tensor", ring(shift))
+        own16 = own.astype(bf)
+        down_gradient = dot(own16[:, rank:], x_rows, ((0,), (0,)))
+        up_gradient = adapter_scale * dot(own16[:, :rank], cot_rows, ((0,), (0,)))
 
         layer_out = (
             base_out + adapter_scale * dot(hidden16, up_all, ((1,), (0,)))

time: 378 us -> 314 us (0.83)
  waiting for transfers between devices: 274 us -> 191 us
  matrix products: 58.3 us -> 71.7 us
  starting transfers between devices: 6.08 us -> 13.1 us
    all_to_all x0 -> x1, waiting for transfers between devices: none -> 127 us  [per_device(): lax.all_to_all(send.reshape(n_owner, -1, feat + keys), 'dp', split_axis=0...]
    reduce_scatter x2 -> x0, waiting for transfers between devices: 123 us -> none  [the longest x1 123 us: per_device(): lax.psum_scatter(down_part, 'dp', scatter_dimension=0, tiled=True)]
    all_gather x1, waiting for transfers between devices: 79.3 us -> 0.01 us  [per_device(): all16 = lax.all_gather(both16, 'dp', axis=0, tiled=True)]
    ppermute x1, waiting for transfers between devices: 14.5 us -> 0.01 us  [per_device(): lax.ppermute(dot(tokens, weights[shift], ((1,), (0,))), 'tensor', ring(-s...]
    dot_general x10 -> x14, matrix products: 58.3 us -> 71.7 us  [dot(): lax.dot_general(a, b, (contract, ((), ())), preferred_element_type=jnp.fl...]
    all_to_all x0 -> x1, starting transfers between devices: none -> 6.56 us  [per_device(): lax.all_to_all(send.reshape(n_owner, -1, feat + keys), 'dp', split_axis=0...]
    concatenate x0 -> x2, other arithmetic: none -> 6.29 us  [the longest x1 6.27 us: per_device(): jnp.concatenate([dot(pick, x, ((1,), (0,))).astype(bf) for x in (tokens,...]
    broadcast_in_dim x3 -> x1, other arithmetic: 6.58 us -> 0.66 us  [owner_masks(): start = jnp.sum(jnp.where(select, lower[None, :], 0), axis=1)]
  transfers between devices with their start and end apart: 8 -> 8, of which waited for: 5 -> 4; matrix products, arithmetic and copies ran while one was open for 15% -> 25% of each run, Pallas kernels for 0% -> 0%
where the time goes in v2:
time: 314 us; the launch traced here: 312 us
  waiting for transfers between devices  191 us (61%)
  matrix products  71.7 us (23%)
  other arithmetic  18.5 us (6%)
  between operations  14.3 us (5%)
  starting transfers between devices  13.1 us (4%)
  local copies, waits for them, and re-layouts  3.85 us (1%)
    all_to_all x1, waiting for transfers between devices, per_device(): lax.all_to_all(send.reshape(n_owner, -1, feat + keys), 'dp', split_axis=0...  127 us
    dot_general x14, matrix products, dot(): lax.dot_general(a, b, (contract, ((), ())), preferred_element_type=jnp.fl...  71.7 us
    ppermute x1, waiting for transfers between devices, per_device(): lax.ppermute(lax.dynamic_slice_in_dim(frozen_key_weight, target * feat +...  45.6 us
    ppermute x1, waiting for transfers between devices, per_device(): summed = summed + lax.ppermute(part, 'tensor', ring(shift))  12.8 us
    all_to_all x1, starting transfers between devices, per_device(): lax.all_to_all(send.reshape(n_owner, -1, feat + keys), 'dp', split_axis=0...  6.56 us
  transfers between devices with their start and end apart: 8, of which 4 were waited for; matrix products, arithmetic and copies ran while one was open for 25% of the time, Pallas kernels for 0%

profile of v2, /device:TPU:11, one launch (start us, length us, event | category | flops | bytes accessed | tf_op | source)
XLA Modules:
  0.0 312.4 jit_solution(3902464925266985443)
XLA Ops:
  7.2 0.9 bitcast_convert_fusion.1
  8.1 1.3 bitcast_convert_fusion
  9.4 0.9 pad_maximum_fusion.6
  12.8 1.7 convolution_convert_fusion.1
  14.5 7.7 %convolution_convert_fusion = bf16[768,4096]{1,0:T(8,128)(2,1)} fusion(bf16[512,4096]{1,0:T(8,128)(2,1)} %param.11, s32[768]{0:T(1024)S(1)} %lt.44, s32[768]{0:T(1024)S(1)} %add.147), kind=kOutput, calls=%fused_computation.8 | convolution fusion | flops 3225550848 | bytes 10491904 | tf_op jit(solution)/shard_map/dot_general | solution.py:52
  22.2 6.3 %pad_maximum_fusion = bf16[768,4608]{1,0:T(8,128)(2,1)} fusion(bf16[768,512]{1,0:T(8,128)(2,1)S(1)} %convolution_convert_fusion.1, bf16[768,4096]{1,0:T(8,128)(2,1)} %convolution_convert_fusion), kind=kLoop, calls=%fused_computation.7 | loop fusion | flops 14155776 | bytes 14155776 | tf_op jit(solution)/shard_map/concatenate | solution.py:86
  28.4 6.6 %all-to-all-start = ((bf16[16,48,4608]{2,1,0:T(8,128)(2,1)}), bf16[16,48,4608]{2,1,0:T(8,128)(2,1)}, u32[]{:S(2)}, u32[]{:S(2)}) async-start(bf16[16,48,4608]{2,1,0:T(8,128)(2,1)} %bitcast.87), calls=%async_computation | async-start | bytes 14155776 | tf_op jit(solution)/shard_map/all_to_all | solution.py:89
  35.0 1.8 constant_dynamic-slice_fusion
  36.8 1.3 collective-permute-start
  38.1 45.6 %collective-permute-done = bf16[2048,512]{1,0:T(8,128)(2,1)S(1)} collective-permute-done((bf16[2048,512]{1,0:T(8,128)(2,1)S(1)}, bf16[2048,512]{1,0:T(8,128)(2,1)S(1)}, u32[]{:S(2)}, u32[]{:S(2)}) %collective-permute-start) | collective-permute-done | bytes 2097184 | tf_op jit(solution)/shard_map/ppermute | solution.py:102
  83.7 1.2 collective-permute-start.1
  84.9 1.2 collective-permute-start.4
  86.5 9.2 %fusion.9 = f32[4096,512]{0,1:T(8,128)} fusion(bf16[512,512]{1,0:T(8,128)(2,1)S(1)} %copy-done.4, bf16[8192,512]{1,0:T(8,128)(2,1)} %param.13, s32[]{:T(128)S(6)} %select_n.49), kind=kOutput, calls=%fused_computation.14 | convolution fusion | flops 2147483648 | bytes 13107204 | tf_op jit(solution)/shard_map/dot_general | solution.py:52
  95.7 5.6 %fusion.19 = f32[512,512]{0,1:T(8,128)} fusion(bf16[512,4096]{1,0:T(8,128)(2,1)S(1)} %copy-done.6, bf16[8192,512]{1,0:T(8,128)(2,1)} %param.13, s32[]{:T(128)S(6)} %select_n.49), kind=kOutput, calls=%fused_computation.32 | convolution fusion | flops 2147483648 | bytes 9437188 | tf_op jit(solution)/shard_map/dot_general | solution.py:52
  101.3 3.8 %broadcast_select_fusion.1 = (bf16[2048,512]{1,0:T(8,128)(2,1)S(1)}, bf16[2048,512]{1,0:T(8,128)(2,1)}) fusion(bf16[2048,512]{1,0:T(8,128)(2,1)} %copy-done.1, bf16[2048,512]{1,0:T(8,128)(2,1)} %collective-permute-done.1, pred[]{:T(512)S(6)} %eq.36), kind=kLoop, calls=%fused_computation.25 | loop fusion | flops 2097152 | bytes 8388609 | tf_op jit(solution)/shard_map/jit(_where)/select_n | solution.py:110
  105.2 127.1 %all-to-all-done = bf16[16,48,4608]{2,1,0:T(8,128)(2,1)} async-done(((bf16[16,48,4608]{2,1,0:T(8,128)(2,1)}), bf16[16,48,4608]{2,1,0:T(8,128)(2,1)}, u32[]{:S(2)}, u32[]{:S(2)}) %all-to-all-start) | async-done | bytes 7077920 | tf_op jit(solution)/shard_map/all_to_all | solution.py:89
  232.2 1.5 convolution_multiply_fusion.1
  233.7 5.0 %fusion.7 = f32[768,64]{0,1:T(8,128)S(1)} fusion(bf16[64,4096]{1,0:T(8,128)(2,1)S(1)} %bitcast_convert_fusion, bf16[768,4608]{1,0:T(8,128)(2,1)} %bitcast.15), kind=kOutput, calls=%fused_computation.11 | convolution fusion | flops 402653184 | bytes 7012352 | tf_op jit(solution)/shard_map/dot_general | solution.py:52
  238.7 1.2 collective-permute-start.5
  240.0 3.4 %fusion.18 = f32[512,512]{0,1:T(8,128)} fusion(bf16[512,4096]{1,0:T(8,128)(2,1)S(1)} %copy-done.7, bf16[2048,512]{1,0:T(8,128)(2,1)S(1)} %copy-done, bf16[2048,512]{1,0:T(8,128)(2,1)S(1)} %get-tuple-element.26), kind=kOutput, calls=%fused_computation.31 | convolution fusion | flops 2155872256 | bytes 9437184 | tf_op jit(solution)/shard_map/dot_general | solution.py:52
  243.6 5.5 %collective-permute-done.5 = f32[768,128]{0,1:T(8,128)S(1)} collective-permute-done((f32[768,128]{0,1:T(8,128)S(1)}, f32[768,128]{0,1:T(8,128)S(1)}, u32[]{:S(2)}, u32[]{:S(2)}) %collective-permute-start.5) | collective-permute-done | bytes 393248 | tf_op jit(solution)/shard_map/ppermute | solution.py:144
  249.2 2.2 fusion.42
  251.4 2.4 bitcast_select_fusion
  254.0 7.5 %bitcast_select_fusion.1 = f32[512,1024]{0,1:T(8,128)S(1)} fusion(bf16[512,4096]{1,0:T(8,128)(2,1)S(1)} %copy-done.8, bf16[1024,4608]{1,0:T(8,128)(2,1)} %all-gather.2.cloned.1.call-done, s32[1024]{0:T(1024)S(1)} %lt.41, s32[1024]{0:T(1024)S(1)} %ge.18), kind=kOutput, calls=%fused_computation.20 | convolution fusion | flops 4297064448 | bytes 14688256 | tf_op jit(solution)/shard_map/dot_general | solution.py:52
  261.8 1.3 collective-permute-start.3
  263.1 7.0 %fusion.36 = (f32[1,64,4096]{2,1,0:T(8,128)}, f32[1,64,4096]{2,1,0:T(8,128)}, f32[1,64,4096]{2,1,0:T(8,128)}) fusion(f32[1,64,4096]{2,1,0:T(8,128)S(1)} %copy-done.9, f32[1,64,4096]{2,1,0:T(8,128)S(1)} %copy-done.10, f32[1,64,4096]{2,1,0:T(8,128)S(1)} %copy-done.3, bf16[768,4608]{1,0:T(8,128)(2,1)} %bitcast.15, bf16[768,128]{0,1:T(8,128)(2,1)S(1)} %add_convert_fusion.2), kind=kOutput, calls=%fused_computation.58 | convolution fusion | flops 405798912 | bytes 12681216 | tf_op jit(solution)/shard_map/dot_general | solution.py:52
  270.0 12.8 %collective-permute-done.3 = f32[512,256]{0,1:T(8,128)S(1)} collective-permute-done((f32[512,256]{0,1:T(8,128)S(1)}, f32[512,256]{0,1:T(8,128)S(1)}, u32[]{:S(2)}, u32[]{:S(2)}) %collective-permute-start.3) | collective-permute-done | bytes 524320 | tf_op jit(solution)/shard_map/ppermute | solution.py:128
  283.0 0.9 bitcast_select_fusion.2
  283.9 6.9 %fusion.1 = f32[512,4096]{1,0:T(8,128)} fusion(bf16[512,1024]{0,1:T(8,128)(2,1)S(1)} %get-tuple-element.36, bf16[1024,4608]{1,0:T(8,128)(2,1)S(1)} %bitcast.89), kind=kOutput, calls=%fused_computation.3 | convolution fusion | flops 4294967296 | bytes 17825792 | tf_op jit(solution)/shard_map/dot_general | solution.py:52
  292.0 1.5 add_convert_fusion
  293.5 1.0 copy.28
  294.5 11.0 %fusion = bf16[512,4096]{1,0:T(8,128)(2,1)} fusion(f32[512,4096]{1,0:T(8,128)} %fusion.1, f32[4096,512]{0,1:T(8,128)} %fusion.9, bf16[512,512]{1,0:T(8,128)(2,1)} %collective-permute-done.4, bf16[2048,512]{1,0:T(8,128)(2,1)} %get-tuple-element.27, bf16[2048,512]{1,0:T(8,128)(2,1)S(1)} %get-tuple-element.26), kind=kOutput, calls=%fused_computation.1 | convolution fusion | flops 2162163712 | bytes 25690112 | tf_op jit(solution)/shard_map/dot_general | solution.py:52
  (59 shorter events, 5.1 us)
Async XLA Ops:
  7.2 244.2 %all-gather.2.cloned.1.call-start = ((), (), s32[]{:S(2)}) async-start(), calls=%async_computation.1 | async-start | bytes 10027008 | tf_op jit(solution)/shard_map/all_gather | solution.py:95
  28.4 203.8 %all-to-all-start = ((bf16[16,48,4608]{2,1,0:T(8,128)(2,1)}), bf16[16,48,4608]{2,1,0:T(8,128)(2,1)}, u32[]{:S(2)}, u32[]{:S(2)}) async-start(bf16[16,48,4608]{2,1,0:T(8,128)(2,1)} %bitcast.87), calls=%async_computation | async-start | bytes 14155776 | tf_op jit(solution)/shard_map/all_to_all | solution.py:89
  35.0 49.9 %copy-start.4 = (bf16[512,512]{1,0:T(8,128)(2,1)S(1)}, bf16[512,512]{1,0:T(8,128)(2,1)}, u32[]{:S(2)}) copy-start(bf16[512,512]{1,0:T(8,128)(2,1)} %param.12) | copy-start | bytes 1572868
  36.8 46.9 %collective-permute-start = (bf16[2048,512]{1,0:T(8,128)(2,1)S(1)}, bf16[2048,512]{1,0:T(8,128)(2,1)S(1)}, u32[]{:S(2)}, u32[]{:S(2)}) collective-permute-start(bf16[2048,512]{1,0:T(8,128)(2,1)S(1)} %constant_dynamic-slice_fusion), channel_id=1, source_target_pairs={{0,1},{1,0},{2,3},{3,2},{4,5},{5,4},{6,7},{7,6},{8,9},{9,8},{10,11... | collective-permute-start | bytes 6291464 | tf_op jit(solution)/shard_map/ppermute | solution.py:102
  83.7 12.0 %copy-start.1 = (bf16[2048,512]{1,0:T(8,128)(2,1)}, bf16[2048,512]{1,0:T(8,128)(2,1)S(1)}, u32[]{:S(2)}) copy-start(bf16[2048,512]{1,0:T(8,128)(2,1)S(1)} %collective-permute-done) | copy-start | bytes 6291460
  83.7 17.6 %collective-permute-start.1 = (bf16[2048,512]{1,0:T(8,128)(2,1)S(1)}, bf16[2048,512]{1,0:T(8,128)(2,1)}, u32[]{:S(2)}, u32[]{:S(2)}) collective-permute-start(bf16[2048,512]{1,0:T(8,128)(2,1)S(1)} %collective-permute-done), channel_id=1, source_target_pairs={{0,2},{2,0},{4,6},{6,4},{8,10},{10,8},{12,14},{14,12},{16,18},{18,... | collective-permute-start | bytes 6291464 | tf_op jit(solution)/shard_map/ppermute | solution.py:107
  84.9 209.6 %collective-permute-start.4 = (bf16[512,512]{1,0:T(8,128)(2,1)S(1)}, bf16[512,512]{1,0:T(8,128)(2,1)}, u32[]{:S(2)}, u32[]{:S(2)}) collective-permute-start(bf16[512,512]{1,0:T(8,128)(2,1)S(1)} %copy-done.4), channel_id=1, source_target_pairs={{0,1},{1,0},{2,3},{3,2},{4,5},{5,4},{6,7},{7,6},{8,9},{9,8},{10,11... | collective-permute-start | bytes 1572872 | tf_op jit(solution)/shard_map/ppermute | solution.py:100
  86.5 9.2 %copy-start.6 = (bf16[512,4096]{1,0:T(8,128)(2,1)S(1)}, bf16[512,4096]{1,0:T(8,128)(2,1)}, u32[]{:S(2)}) copy-start(bf16[512,4096]{1,0:T(8,128)(2,1)} %param.11) | copy-start | bytes 12582916
  233.7 6.3 %copy-start = (bf16[2048,512]{1,0:T(8,128)(2,1)S(1)}, bf16[2048,512]{1,0:T(8,128)(2,1)}, u32[]{:S(2)}) copy-start(bf16[2048,512]{1,0:T(8,128)(2,1)} %get-tuple-element.27) | copy-start | bytes 6291460
  233.7 6.3 %copy-start.7 = (bf16[512,4096]{1,0:T(8,128)(2,1)S(1)}, bf16[512,4096]{1,0:T(8,128)(2,1)}, u32[]{:S(2)}) copy-start(bf16[512,4096]{1,0:T(8,128)(2,1)} %param.11) | copy-start | bytes 12582916
  238.7 10.4 %collective-permute-start.5 = (f32[768,128]{0,1:T(8,128)S(1)}, f32[768,128]{0,1:T(8,128)S(1)}, u32[]{:S(2)}, u32[]{:S(2)}) collective-permute-start(f32[768,128]{0,1:T(8,128)S(1)} %pad_maximum_fusion.8), channel_id=1, source_target_pairs={{0,1},{1,0},{2,3},{3,2},{4,5},{5,4},{6,7},{7,6},{8,9},{9,8},{10,11... | collective-permute-start | bytes 1179656 | tf_op jit(solution)/shard_map/ppermute | solution.py:144
  240.0 9.2 %copy-start.5 = (f32[1,64,512]{2,1,0:T(8,128)S(1)}, f32[1,64,512]{2,1,0:T(8,128)}, u32[]{:S(2)}) copy-start(f32[1,64,512]{2,1,0:T(8,128)} %param.17) | copy-start | bytes 393220
  240.0 9.2 %copy-start.11 = (f32[1,64,512]{2,1,0:T(8,128)S(1)}, f32[1,64,512]{2,1,0:T(8,128)}, u32[]{:S(2)}) copy-start(f32[1,64,512]{2,1,0:T(8,128)} %param.21) | copy-start | bytes 393220
  240.0 9.2 %copy-start.12 = (f32[1,64,512]{2,1,0:T(8,128)S(1)}, f32[1,64,512]{2,1,0:T(8,128)}, u32[]{:S(2)}) copy-start(f32[1,64,512]{2,1,0:T(8,128)} %param.20) | copy-start | bytes 393220
  243.4 48.2 %collective-permute-start.2 = (f32[512,512]{0,1:T(8,128)}, f32[512,512]{0,1:T(8,128)}, u32[]{:S(2)}, u32[]{:S(2)}) collective-permute-start(f32[512,512]{0,1:T(8,128)} %fusion.18), channel_id=1, source_target_pairs={{0,1},{1,0},{2,3},{3,2},{4,5},{5,4},{6,7},{7,6},{8,9},{9,8},{10,11... | collective-permute-start | bytes 3145736 | tf_op jit(solution)/shard_map/ppermute | solution.py:117
  251.4 2.6 copy-start.8
  254.0 9.1 %copy-start.3 = (f32[1,64,4096]{2,1,0:T(8,128)S(1)}, f32[1,64,4096]{2,1,0:T(8,128)}, u32[]{:S(2)}) copy-start(f32[1,64,4096]{2,1,0:T(8,128)} %param.16) | copy-start | bytes 3145732
  254.0 9.1 %copy-start.9 = (f32[1,64,4096]{2,1,0:T(8,128)S(1)}, f32[1,64,4096]{2,1,0:T(8,128)}, u32[]{:S(2)}) copy-start(f32[1,64,4096]{2,1,0:T(8,128)} %param.19) | copy-start | bytes 3145732
  254.0 9.1 %copy-start.10 = (f32[1,64,4096]{2,1,0:T(8,128)S(1)}, f32[1,64,4096]{2,1,0:T(8,128)}, u32[]{:S(2)}) copy-start(f32[1,64,4096]{2,1,0:T(8,128)} %param.18) | copy-start | bytes 3145732
  261.8 22.1 %slice-start = ((s8[9437184]{0:T(1024)(128)(4,1)}), s8[4194304]{0:T(1024)(128)(4,1)S(1)}, s32[]{:S(2)}) async-start(s8[9437184]{0:T(1024)(128)(4,1)} %bitcast.88), calls=%async_computation.2 | async-start | bytes 8388608
  261.8 22.0 %slice-start.1 = ((s8[9437184]{0:T(1024)(128)(4,1)}), s8[4194304]{0:T(1024)(128)(4,1)S(1)}, s32[]{:S(2)}) async-start(s8[9437184]{0:T(1024)(128)(4,1)} %bitcast.88), calls=%async_computation.3 | async-start | bytes 8388608
  261.8 22.0 %slice-start.2 = ((s8[9437184]{0:T(1024)(128)(4,1)}), s8[1048576]{0:T(1024)(128)(4,1)S(1)}, s32[]{:S(2)}) async-start(s8[9437184]{0:T(1024)(128)(4,1)} %bitcast.88), calls=%async_computation.4 | async-start | bytes 2097152
  261.8 21.0 %collective-permute-start.3 = (f32[512,256]{0,1:T(8,128)S(1)}, f32[512,256]{0,1:T(8,128)S(1)}, u32[]{:S(2)}, u32[]{:S(2)}) collective-permute-start(f32[512,256]{0,1:T(8,128)S(1)} %pad_maximum_fusion.7), channel_id=1, source_target_pairs={{0,1},{1,0},{2,3},{3,2},{4,5},{5,4},{6,7},{7,6},{8,9},{9,8},{10,11... | collective-permute-start | bytes 1572872 | tf_op jit(solution)/shard_map/ppermute | solution.py:128
  290.8 1.2 copy-start.2
Sparse Core Ops, SparseCore 0:
  10.9 174.9 all-gather.1

commit v3 on v2

--- a/solution.py
+++ b/solution.py
@@ -131,6 +131,15 @@
         hidden16 = jnp.where(mask, jnp.tile(summed[:, :width].astype(bf), (1, times)), zero)
         back16 = jnp.where(mask, jnp.tile(summed[:, width:].astype(bf), (1, times)), zero)
 
+        layer_out = (
+            base_out + adapter_scale * dot(hidden16, up_all, ((1,), (0,)))
+        ).astype(bf)
+        base_grad = dot(back16, down_all, ((1,), (0,)))
+        for cot, weight in zip(cots, weights):
+            base_grad = base_grad + dot(cot, weight, ((1,), (1,)))
+        input_grad = base_grad.astype(bf)
+        routed, layer_out, input_grad = lax.optimization_barrier((routed, layer_out, input_grad))
+
         x_rows, cot_rows = routed[:, :feat], routed[:, feat:]
         own_part = jnp.concatenate(
             [
@@ -146,13 +155,6 @@
         down_gradient = dot(own16[:, rank:], x_rows, ((0,), (0,)))
         up_gradient = adapter_scale * dot(own16[:, :rank], cot_rows, ((0,), (0,)))
 
-        layer_out = (
-            base_out + adapter_scale * dot(hidden16, up_all, ((1,), (0,)))
-        ).astype(bf)
-        base_grad = dot(back16, down_all, ((1,), (0,)))
-        for cot, weight in zip(cots, weights):
-            base_grad = base_grad + dot(cot, weight, ((1,), (1,)))
-        input_grad = base_grad.astype(bf)
         fresh_down = optimizer_update(
             adapter_down_matrix[0], down_first_moment[0], down_second_moment[0], down_gradient
         )

time: 314 us -> 285 us (0.908)
  the two profiles are of different devices: /device:TPU:11 before, /device:TPU:28 now
where the time goes in v3:
time: 285 us
  waiting for transfers between devices  171 us (60%)
  matrix products  69.5 us (24%)
  other arithmetic  17.2 us (6%)
  between operations  14.3 us (5%)
  starting transfers between devices  9.69 us (3%)
  local copies, waits for them, and re-layouts  3.31 us (1%)
    all_gather x1, waiting for transfers between devices, per_device(): all16 = lax.all_gather(both16, 'dp', axis=0, tiled=True)  92.4 us
    dot_general x14, matrix products, dot(): lax.dot_general(a, b, (contract, ((), ())), preferred_element_type=jnp.fl...  69.5 us
    ppermute x1, waiting for transfers between devices, per_device(): lax.ppermute(lax.dynamic_slice_in_dim(frozen_key_weight, target * feat +...  47.2 us
    ppermute x1, waiting for transfers between devices, per_device(): lax.ppermute(dot(tokens, weights[shift], ((1,), (0,))), 'tensor', ring(-s...  12.8 us
    ppermute x1, waiting for transfers between devices, per_device(): summed = summed + lax.ppermute(part, 'tensor', ring(shift))  9.33 us
    ppermute x1, waiting for transfers between devices, per_device(): own = own + lax.ppermute(own_part, 'tensor', ring(shift))  9.11 us
    concatenate x1, other arithmetic, per_device(): jnp.concatenate([dot(pick, x, ((1,), (0,))).astype(bf) for x in (tokens,...  6.17 us
    all_to_all x1, starting transfers between devices, per_device(): lax.all_to_all(send.reshape(n_owner, -1, feat + keys), 'dp', split_axis=0...  6.05 us
  transfers between devices with their start and end apart: 8, of which 5 were waited for; matrix products, arithmetic and copies ran while one was open for 25% of the time, Pallas kernels for 0%

profile of v3, /device:TPU:28, one launch (start us, length us, event | category | flops | bytes accessed | tf_op | source)
XLA Modules:
  0.0 284.8 jit_solution(6609353697996128993)
XLA Ops:
  7.2 0.9 bitcast_convert_fusion.1
  8.1 1.3 bitcast_convert_fusion
  9.4 0.9 pad_maximum_fusion.6
  10.3 0.8 select_reduce_fusion.2
  11.1 0.7 fusion.43
  11.7 0.8 select_reduce_fusion.1
  12.8 1.7 convolution_convert_fusion.1
  14.5 7.7 %convolution_convert_fusion = bf16[768,4096]{1,0:T(8,128)(2,1)} fusion(bf16[512,4096]{1,0:T(8,128)(2,1)} %param.11, s32[768]{0:T(1024)S(1)} %lt.38, s32[768]{0:T(1024)S(1)} %add.123), kind=kOutput, calls=%fused_computation.8 | convolution fusion | flops 3225550848 | bytes 10491904 | tf_op jit(solution)/shard_map/dot_general | solution.py:52
  22.2 6.2 %pad_maximum_fusion = bf16[768,4608]{1,0:T(8,128)(2,1)} fusion(bf16[768,512]{1,0:T(8,128)(2,1)S(1)} %convolution_convert_fusion.1, bf16[768,4096]{1,0:T(8,128)(2,1)} %convolution_convert_fusion), kind=kLoop, calls=%fused_computation.7 | loop fusion | flops 14155776 | bytes 14155776 | tf_op jit(solution)/shard_map/concatenate | solution.py:86
  28.4 6.0 %all-to-all-start = ((bf16[16,48,4608]{2,1,0:T(8,128)(2,1)}), bf16[16,48,4608]{2,1,0:T(8,128)(2,1)}, u32[]{:S(2)}, u32[]{:S(2)}) async-start(bf16[16,48,4608]{2,1,0:T(8,128)(2,1)} %bitcast.89), calls=%async_computation | async-start | bytes 14155776 | tf_op jit(solution)/shard_map/all_to_all | solution.py:89
  34.4 1.7 constant_dynamic-slice_fusion
  36.7 47.2 %collective-permute-done = bf16[2048,512]{1,0:T(8,128)(2,1)S(1)} collective-permute-done((bf16[2048,512]{1,0:T(8,128)(2,1)S(1)}, bf16[2048,512]{1,0:T(8,128)(2,1)S(1)}, u32[]{:S(2)}, u32[]{:S(2)}) %collective-permute-start) | collective-permute-done | bytes 2097184 | tf_op jit(solution)/shard_map/ppermute | solution.py:102
  84.7 8.3 %fusion.9 = f32[4096,512]{0,1:T(8,128)} fusion(bf16[512,512]{1,0:T(8,128)(2,1)} %param.12, bf16[8192,512]{1,0:T(8,128)(2,1)} %param.13, s32[]{:T(128)S(6)} %select_n.52), kind=kOutput, calls=%fused_computation.14 | convolution fusion | flops 2147483648 | bytes 13107204 | tf_op jit(solution)/shard_map/dot_general | solution.py:52
  93.0 5.6 %fusion.19 = f32[512,512]{0,1:T(8,128)} fusion(bf16[512,4096]{1,0:T(8,128)(2,1)S(1)} %copy-done.5, bf16[8192,512]{1,0:T(8,128)(2,1)} %param.13, s32[]{:T(128)S(6)} %select_n.52), kind=kOutput, calls=%fused_computation.32 | convolution fusion | flops 2147483648 | bytes 9437188 | tf_op jit(solution)/shard_map/dot_general | solution.py:52
  98.6 3.8 %broadcast_select_fusion.1 = (bf16[2048,512]{1,0:T(8,128)(2,1)S(1)}, bf16[2048,512]{1,0:T(8,128)(2,1)}) fusion(bf16[2048,512]{1,0:T(8,128)(2,1)} %copy-done.1, bf16[2048,512]{1,0:T(8,128)(2,1)} %collective-permute-done.1, pred[]{:T(512)S(6)} %eq.44), kind=kLoop, calls=%fused_computation.25 | loop fusion | flops 2097152 | bytes 8388609 | tf_op jit(solution)/shard_map/jit(_where)/select_n | solution.py:110
  102.4 92.4 %all-gather.2.cloned.1.call-done = bf16[1024,4608]{1,0:T(8,128)(2,1)} async-done(((bf16[64,4608]{1,0:T(8,128)(2,1)}), bf16[1024,4608]{1,0:T(8,128)(2,1)}) %all-gather.2.cloned.1.call-update) | async-done | bytes 9437200 | tf_op jit(solution)/shard_map/all_gather | solution.py:95
  194.9 2.5 bitcast_select_fusion
  197.6 7.3 %bitcast_select_fusion.1 = f32[512,1024]{0,1:T(8,128)S(1)} fusion(bf16[512,4096]{1,0:T(8,128)(2,1)S(1)} %copy-done.6, bf16[1024,4608]{1,0:T(8,128)(2,1)} %all-gather.2.cloned.1.call-done, s32[1024]{0:T(1024)S(1)} %lt.44, s32[1024]{0:T(1024)S(1)} %ge.18), kind=kOutput, calls=%fused_computation.20 | convolution fusion | flops 4297064448 | bytes 14688256 | tf_op jit(solution)/shard_map/dot_general | solution.py:52
  205.6 3.4 %fusion.18 = f32[512,512]{0,1:T(8,128)} fusion(bf16[512,4096]{1,0:T(8,128)(2,1)S(1)} %copy-done.6, bf16[2048,512]{1,0:T(8,128)(2,1)S(1)} %copy-done, bf16[2048,512]{1,0:T(8,128)(2,1)S(1)} %get-tuple-element.32), kind=kOutput, calls=%fused_computation.31 | convolution fusion | flops 2155872256 | bytes 9437184 | tf_op jit(solution)/shard_map/dot_general | solution.py:52
  209.0 1.7 collective-permute-start.2
  210.7 9.3 %collective-permute-done.3 = f32[512,256]{0,1:T(8,128)S(1)} collective-permute-done((f32[512,256]{0,1:T(8,128)S(1)}, f32[512,256]{0,1:T(8,128)S(1)}, u32[]{:S(2)}, u32[]{:S(2)}) %collective-permute-start.3) | collective-permute-done | bytes 524320 | tf_op jit(solution)/shard_map/ppermute | solution.py:128
  220.1 0.9 bitcast_select_fusion.2
  221.1 7.2 %fusion.1 = f32[512,4096]{1,0:T(8,128)} fusion(bf16[512,1024]{0,1:T(8,128)(2,1)S(1)} %get-tuple-element.42, bf16[1024,4608]{1,0:T(8,128)(2,1)S(1)} %bitcast.91), kind=kOutput, calls=%fused_computation.3 | convolution fusion | flops 4294967296 | bytes 17825792 | tf_op jit(solution)/shard_map/dot_general | solution.py:52
  228.3 0.8 convolution_multiply_fusion
  229.0 12.8 %collective-permute-done.2 = f32[512,512]{0,1:T(8,128)S(1)} collective-permute-done((f32[512,512]{0,1:T(8,128)}, f32[512,512]{0,1:T(8,128)S(1)}, u32[]{:S(2)}, u32[]{:S(2)}) %collective-permute-start.2) | collective-permute-done | bytes 1048608 | tf_op jit(solution)/shard_map/ppermute | solution.py:117
  242.3 9.6 %fusion = bf16[512,4096]{1,0:T(8,128)(2,1)} fusion(f32[512,4096]{1,0:T(8,128)} %fusion.1, f32[4096,512]{0,1:T(8,128)S(1)} %bitcast.88, bf16[512,512]{1,0:T(8,128)(2,1)} %collective-permute-done.4, bf16[2048,512]{1,0:T(8,128)(2,1)S(1)} %copy-done, bf16[2048,512]{1,0:T(8,128)(2,1)S(1)} %get-tuple-element.32), kind=kOutput, calls=%fused_computation.1 | convolution fusion | flops 2162163712 | bytes 25690112 | tf_op jit(solution)/shard_map/dot_general | solution.py:52
  251.9 4.9 %fusion.7 = f32[768,64]{0,1:T(8,128)S(1)} fusion(bf16[64,4096]{1,0:T(8,128)(2,1)S(1)} %bitcast_convert_fusion, bf16[768,4608]{1,0:T(8,128)(2,1)} %bitcast.4), kind=kOutput, calls=%fused_computation.11 | convolution fusion | flops 402653184 | bytes 7012352 | tf_op jit(solution)/shard_map/dot_general | solution.py:52
  256.7 1.6 convolution_multiply_fusion.1
  258.8 1.0 copy.28
  259.8 9.1 %collective-permute-done.5 = f32[768,128]{0,1:T(8,128)S(1)} collective-permute-done((f32[768,128]{0,1:T(8,128)S(1)}, f32[768,128]{0,1:T(8,128)S(1)}, u32[]{:S(2)}, u32[]{:S(2)}) %collective-permute-start.5) | collective-permute-done | bytes 393248 | tf_op jit(solution)/shard_map/ppermute | solution.py:153
  269.0 2.2 fusion.42
  271.2 6.8 %fusion.36 = (f32[1,64,4096]{2,1,0:T(8,128)}, f32[1,64,4096]{2,1,0:T(8,128)}, f32[1,64,4096]{2,1,0:T(8,128)}) fusion(f32[1,64,4096]{2,1,0:T(8,128)} %param.19, f32[1,64,4096]{2,1,0:T(8,128)} %param.18, f32[1,64,4096]{2,1,0:T(8,128)S(1)} %copy-done.3, bf16[768,4608]{1,0:T(8,128)(2,1)} %bitcast.4, bf16[768,128]{0,1:T(8,128)(2,1)S(1)} %add_convert_fusion.2), kind=kOutput, calls=%fused_computation.58 | convolution fusion | flops 405798912 | bytes 12681216 | tf_op jit(solution)/shard_map/dot_general | solution.py:52
  (54 shorter events, 3.7 us)
Async XLA Ops:
  7.2 187.7 %all-gather.2.cloned.1.call-start = ((), (), s32[]{:S(2)}) async-start(), calls=%async_computation.1 | async-start | bytes 10027008 | tf_op jit(solution)/shard_map/all_gather | solution.py:95
  28.4 223.5 %all-to-all-start = ((bf16[16,48,4608]{2,1,0:T(8,128)(2,1)}), bf16[16,48,4608]{2,1,0:T(8,128)(2,1)}, u32[]{:S(2)}, u32[]{:S(2)}) async-start(bf16[16,48,4608]{2,1,0:T(8,128)(2,1)} %bitcast.89), calls=%async_computation | async-start | bytes 14155776 | tf_op jit(solution)/shard_map/all_to_all | solution.py:89
  36.1 47.8 %collective-permute-start = (bf16[2048,512]{1,0:T(8,128)(2,1)S(1)}, bf16[2048,512]{1,0:T(8,128)(2,1)S(1)}, u32[]{:S(2)}, u32[]{:S(2)}) collective-permute-start(bf16[2048,512]{1,0:T(8,128)(2,1)S(1)} %constant_dynamic-slice_fusion), channel_id=1, source_target_pairs={{0,1},{1,0},{2,3},{3,2},{4,5},{5,4},{6,7},{7,6},{8,9},{9,8},{10,11... | collective-permute-start | bytes 6291464 | tf_op jit(solution)/shard_map/ppermute | solution.py:102
  83.9 9.1 %copy-start.1 = (bf16[2048,512]{1,0:T(8,128)(2,1)}, bf16[2048,512]{1,0:T(8,128)(2,1)S(1)}, u32[]{:S(2)}) copy-start(bf16[2048,512]{1,0:T(8,128)(2,1)S(1)} %collective-permute-done) | copy-start | bytes 6291460
  83.9 14.7 %collective-permute-start.1 = (bf16[2048,512]{1,0:T(8,128)(2,1)S(1)}, bf16[2048,512]{1,0:T(8,128)(2,1)}, u32[]{:S(2)}, u32[]{:S(2)}) collective-permute-start(bf16[2048,512]{1,0:T(8,128)(2,1)S(1)} %collective-permute-done), channel_id=1, source_target_pairs={{0,2},{2,0},{4,6},{6,4},{8,10},{10,8},{12,14},{14,12},{16,18},{18,... | collective-permute-start | bytes 6291464 | tf_op jit(solution)/shard_map/ppermute | solution.py:107
  83.9 158.3 %collective-permute-start.4 = (bf16[512,512]{1,0:T(8,128)(2,1)}, bf16[512,512]{1,0:T(8,128)(2,1)}, u32[]{:S(2)}, u32[]{:S(2)}) collective-permute-start(bf16[512,512]{1,0:T(8,128)(2,1)} %param.12), channel_id=1, source_target_pairs={{0,1},{1,0},{2,3},{3,2},{4,5},{5,4},{6,7},{7,6},{8,9},{9,8},{10,11... | collective-permute-start | bytes 1572872 | tf_op jit(solution)/shard_map/ppermute | solution.py:100
  84.7 8.3 %copy-start.5 = (bf16[512,4096]{1,0:T(8,128)(2,1)S(1)}, bf16[512,4096]{1,0:T(8,128)(2,1)}, u32[]{:S(2)}) copy-start(bf16[512,4096]{1,0:T(8,128)(2,1)} %param.11) | copy-start | bytes 12582916
  194.9 2.8 copy-start.6
  197.6 8.0 %copy-start = (bf16[2048,512]{1,0:T(8,128)(2,1)S(1)}, bf16[2048,512]{1,0:T(8,128)(2,1)}, u32[]{:S(2)}) copy-start(bf16[2048,512]{1,0:T(8,128)(2,1)} %get-tuple-element.33) | copy-start | bytes 6291460
  205.2 14.8 %collective-permute-start.3 = (f32[512,256]{0,1:T(8,128)S(1)}, f32[512,256]{0,1:T(8,128)S(1)}, u32[]{:S(2)}, u32[]{:S(2)}) collective-permute-start(f32[512,256]{0,1:T(8,128)S(1)} %pad_maximum_fusion.7), channel_id=1, source_target_pairs={{0,1},{1,0},{2,3},{3,2},{4,5},{5,4},{6,7},{7,6},{8,9},{9,8},{10,11... | collective-permute-start | bytes 1572872 | tf_op jit(solution)/shard_map/ppermute | solution.py:128
  205.6 15.4 %slice-start.2 = ((s8[9437184]{0:T(1024)(128)(4,1)}), s8[4194304]{0:T(1024)(128)(4,1)S(1)}, s32[]{:S(2)}) async-start(s8[9437184]{0:T(1024)(128)(4,1)} %bitcast.90), calls=%async_computation.4 | async-start | bytes 8388608
  205.6 15.4 %slice-start.3 = ((s8[9437184]{0:T(1024)(128)(4,1)}), s8[4194304]{0:T(1024)(128)(4,1)S(1)}, s32[]{:S(2)}) async-start(s8[9437184]{0:T(1024)(128)(4,1)} %bitcast.90), calls=%async_computation.5 | async-start | bytes 8388608
  205.6 15.4 %slice-start.4 = ((s8[9437184]{0:T(1024)(128)(4,1)}), s8[1048576]{0:T(1024)(128)(4,1)S(1)}, s32[]{:S(2)}) async-start(s8[9437184]{0:T(1024)(128)(4,1)} %bitcast.90), calls=%async_computation.6 | async-start | bytes 2097152
  209.0 32.8 %collective-permute-start.2 = (f32[512,512]{0,1:T(8,128)}, f32[512,512]{0,1:T(8,128)S(1)}, u32[]{:S(2)}, u32[]{:S(2)}) collective-permute-start(f32[512,512]{0,1:T(8,128)} %fusion.18), channel_id=1, source_target_pairs={{0,1},{1,0},{2,3},{3,2},{4,5},{5,4},{6,7},{7,6},{8,9},{9,8},{10,11... | collective-permute-start | bytes 3145736 | tf_op jit(solution)/shard_map/ppermute | solution.py:117
  221.0 21.2 %slice-start = ((s8[8388608]{0:T(1024)(128)(4,1)}), s8[4194304]{0:T(1024)(128)(4,1)S(1)}, s32[]{:S(2)}) async-start(s8[8388608]{0:T(1024)(128)(4,1)} %bitcast.87), calls=%async_computation.2 | async-start | bytes 8388608
  221.1 21.2 %slice-start.1 = ((s8[8388608]{0:T(1024)(128)(4,1)}), s8[4194304]{0:T(1024)(128)(4,1)S(1)}, s32[]{:S(2)}) async-start(s8[8388608]{0:T(1024)(128)(4,1)} %bitcast.87), calls=%async_computation.3 | async-start | bytes 8388608
  228.3 13.6 %copy-start.2 = (f32[512,512]{0,1:T(8,128)S(1)}, f32[512,512]{0,1:T(8,128)}, u32[]{:S(2)}) copy-start(f32[512,512]{0,1:T(8,128)} %fusion.19) | copy-start | bytes 3145732
  251.9 17.1 %copy-start.4 = (f32[1,64,512]{2,1,0:T(8,128)S(1)}, f32[1,64,512]{2,1,0:T(8,128)}, u32[]{:S(2)}) copy-start(f32[1,64,512]{2,1,0:T(8,128)} %param.17) | copy-start | bytes 393220
  251.9 17.1 %copy-start.7 = (f32[1,64,512]{2,1,0:T(8,128)S(1)}, f32[1,64,512]{2,1,0:T(8,128)}, u32[]{:S(2)}) copy-start(f32[1,64,512]{2,1,0:T(8,128)} %param.21) | copy-start | bytes 393220
  256.7 14.5 %copy-start.3 = (f32[1,64,4096]{2,1,0:T(8,128)S(1)}, f32[1,64,4096]{2,1,0:T(8,128)}, u32[]{:S(2)}) copy-start(f32[1,64,4096]{2,1,0:T(8,128)} %param.16) | copy-start | bytes 3145732
  258.3 10.5 %collective-permute-start.5 = (f32[768,128]{0,1:T(8,128)S(1)}, f32[768,128]{0,1:T(8,128)S(1)}, u32[]{:S(2)}, u32[]{:S(2)}) collective-permute-start(f32[768,128]{0,1:T(8,128)S(1)} %pad_maximum_fusion.8), channel_id=1, source_target_pairs={{0,1},{1,0},{2,3},{3,2},{4,5},{5,4},{6,7},{7,6},{8,9},{9,8},{10,11... | collective-permute-start | bytes 1179656 | tf_op jit(solution)/shard_map/ppermute | solution.py:153
Sparse Core Ops, SparseCore 0:
  10.9 183.9 all-gather.1

commit v4 on v2

--- a/solution.py
+++ b/solution.py
@@ -118,6 +118,7 @@
                 dot(tokens, weights[shift], ((1,), (0,))), "tensor", ring(-shift)
             )
 
+        all16, base_out = lax.optimization_barrier((all16, base_out))
         down_all = all16[:, :feat]
         up_all = all16[:, feat:]
         hidden_part = fold(jnp.where(mask, dot(tokens, down_all, ((1,), (1,))), 0.0), width)
@@ -131,6 +132,7 @@
         hidden16 = jnp.where(mask, jnp.tile(summed[:, :width].astype(bf), (1, times)), zero)
         back16 = jnp.where(mask, jnp.tile(summed[:, width:].astype(bf), (1, times)), zero)
 
+        routed, hidden16, back16 = lax.optimization_barrier((routed, hidden16, back16))
         x_rows, cot_rows = routed[:, :feat], routed[:, feat:]
         own_part = jnp.concatenate(
             [

time: 314 us -> 280 us (0.89)
  waiting for transfers between devices: 191 us -> 157 us
    all_to_all x1, waiting for transfers between devices: 127 us -> 23.8 us  [per_device(): lax.all_to_all(send.reshape(n_owner, -1, feat + keys), 'dp', split_axis=0...]
    all_gather x1, waiting for transfers between devices: 0.01 us -> 61.6 us  [per_device(): all16 = lax.all_gather(both16, 'dp', axis=0, tiled=True)]
    ppermute x1, waiting for transfers between devices: 0.01 us -> 17.3 us  [per_device(): lax.ppermute(dot(tokens, weights[shift], ((1,), (0,))), 'tensor', ring(-s...]
    ppermute x1, waiting for transfers between devices: 12.8 us -> 4.96 us  [per_device(): summed = summed + lax.ppermute(part, 'tensor', ring(shift))]
    ppermute x1, waiting for transfers between devices: 5.45 us -> 0.01 us  [per_device(): own = own + lax.ppermute(own_part, 'tensor', ring(shift))]
    ppermute x1, waiting for transfers between devices: 0.01 us -> 3.82 us  [per_device(): got_peer = lax.ppermute(got, 'dp', swap_core)]
  transfers between devices with their start and end apart: 8 -> 8, of which waited for: 4 -> 6; matrix products, arithmetic and copies ran while one was open for 25% -> 29% of each run, Pallas kernels for 0% -> 0%
where the time goes in v4:
time: 280 us
  waiting for transfers between devices  157 us (56%)
  matrix products  73.3 us (26%)
  other arithmetic  17.7 us (6%)
  between operations  14.3 us (5%)
  starting transfers between devices  13.2 us (5%)
  local copies, waits for them, and re-layouts  4.23 us (2%)
    dot_general x14, matrix products, dot(): lax.dot_general(a, b, (contract, ((), ())), preferred_element_type=jnp.fl...  73.3 us
    all_gather x1, waiting for transfers between devices, per_device(): all16 = lax.all_gather(both16, 'dp', axis=0, tiled=True)  61.6 us
    ppermute x1, waiting for transfers between devices, per_device(): lax.ppermute(lax.dynamic_slice_in_dim(frozen_key_weight, target * feat +...  45.6 us
    all_to_all x1, waiting for transfers between devices, per_device(): lax.all_to_all(send.reshape(n_owner, -1, feat + keys), 'dp', split_axis=0...  23.8 us
    ppermute x1, waiting for transfers between devices, per_device(): lax.ppermute(dot(tokens, weights[shift], ((1,), (0,))), 'tensor', ring(-s...  17.3 us
    all_to_all x1, starting transfers between devices, per_device(): lax.all_to_all(send.reshape(n_owner, -1, feat + keys), 'dp', split_axis=0...  6.57 us
    concatenate x1, other arithmetic, per_device(): jnp.concatenate([dot(pick, x, ((1,), (0,))).astype(bf) for x in (tokens,...  6.18 us
  transfers between devices with their start and end apart: 8, of which 6 were waited for; matrix products, arithmetic and copies ran while one was open for 29% of the time, Pallas kernels for 0%

profile of v4, /device:TPU:11, one launch (start us, length us, event | category | flops | bytes accessed | tf_op | source)
XLA Modules:
  0.0 279.9 jit_solution(11723062170073584412)
XLA Ops:
  8.1 1.3 bitcast_convert_fusion
  13.6 1.7 convolution_convert_fusion.1
  15.3 7.7 %convolution_convert_fusion = bf16[768,4096]{1,0:T(8,128)(2,1)} fusion(bf16[512,4096]{1,0:T(8,128)(2,1)} %param.11, s32[768]{0:T(1024)S(1)} %lt.41, s32[768]{0:T(1024)S(1)} %add.129), kind=kOutput, calls=%fused_computation.8 | convolution fusion | flops 3225550848 | bytes 10491904 | tf_op jit(solution)/shard_map/dot_general | solution.py:52
  23.0 6.2 %pad_maximum_fusion = bf16[768,4608]{1,0:T(8,128)(2,1)} fusion(bf16[768,512]{1,0:T(8,128)(2,1)S(1)} %convolution_convert_fusion.1, bf16[768,4096]{1,0:T(8,128)(2,1)} %convolution_convert_fusion), kind=kLoop, calls=%fused_computation.7 | loop fusion | flops 14155776 | bytes 14155776 | tf_op jit(solution)/shard_map/concatenate | solution.py:86
  29.2 6.6 %all-to-all-start = ((bf16[16,48,4608]{2,1,0:T(8,128)(2,1)}), bf16[16,48,4608]{2,1,0:T(8,128)(2,1)}, u32[]{:S(2)}, u32[]{:S(2)}) async-start(bf16[16,48,4608]{2,1,0:T(8,128)(2,1)} %bitcast.89), calls=%async_computation | async-start | bytes 14155776 | tf_op jit(solution)/shard_map/all_to_all | solution.py:89
  35.7 1.7 constant_dynamic-slice_fusion
  37.5 1.3 collective-permute-start
  38.8 45.6 %collective-permute-done = bf16[2048,512]{1,0:T(8,128)(2,1)S(1)} collective-permute-done((bf16[2048,512]{1,0:T(8,128)(2,1)S(1)}, bf16[2048,512]{1,0:T(8,128)(2,1)S(1)}, u32[]{:S(2)}, u32[]{:S(2)}) %collective-permute-start) | collective-permute-done | bytes 2097184 | tf_op jit(solution)/shard_map/ppermute | solution.py:102
  84.4 1.2 collective-permute-start.1
  85.7 3.8 %collective-permute-done.1 = bf16[2048,512]{1,0:T(8,128)(2,1)} collective-permute-done((bf16[2048,512]{1,0:T(8,128)(2,1)S(1)}, bf16[2048,512]{1,0:T(8,128)(2,1)}, u32[]{:S(2)}, u32[]{:S(2)}) %collective-permute-start.1) | collective-permute-done | bytes 2097184 | tf_op jit(solution)/shard_map/ppermute | solution.py:107
  89.5 2.5 broadcast_select_fusion.1
  92.0 3.3 %fusion.18 = f32[512,512]{0,1:T(8,128)} fusion(bf16[512,4096]{1,0:T(8,128)(2,1)S(1)} %copy-done.9, bf16[2048,512]{1,0:T(8,128)(2,1)S(1)} %get-tuple-element.37, bf16[2048,512]{1,0:T(8,128)(2,1)S(1)} %get-tuple-element.36), kind=kOutput, calls=%fused_computation.31 | convolution fusion | flops 2155872256 | bytes 9437184 | tf_op jit(solution)/shard_map/dot_general | solution.py:52
  95.4 1.2 collective-permute-start.2
  96.9 5.8 %fusion.19 = f32[512,512]{0,1:T(8,128)S(1)} fusion(bf16[512,4096]{1,0:T(8,128)(2,1)} %param.11, bf16[8192,512]{1,0:T(8,128)(2,1)} %param.13, s32[]{:T(128)S(6)} %select_n.49), kind=kOutput, calls=%fused_computation.32 | convolution fusion | flops 2147483648 | bytes 9437188 | tf_op jit(solution)/shard_map/dot_general | solution.py:52
  102.8 17.3 %collective-permute-done.2 = f32[512,512]{0,1:T(8,128)S(1)} collective-permute-done((f32[512,512]{0,1:T(8,128)}, f32[512,512]{0,1:T(8,128)S(1)}, u32[]{:S(2)}, u32[]{:S(2)}) %collective-permute-start.2) | collective-permute-done | bytes 1048608 | tf_op jit(solution)/shard_map/ppermute | solution.py:117
  120.1 1.2 add.125
  121.2 61.6 %all-gather.2.cloned.1.call-done = bf16[1024,4608]{1,0:T(8,128)(2,1)} async-done(((bf16[64,4608]{1,0:T(8,128)(2,1)}), bf16[1024,4608]{1,0:T(8,128)(2,1)}) %all-gather.2.cloned.1.call-update) | async-done | bytes 9437200 | tf_op jit(solution)/shard_map/all_gather | solution.py:95
  182.9 2.5 bitcast_select_fusion
  185.7 7.7 %bitcast_select_fusion.1 = f32[512,1024]{0,1:T(8,128)S(1)} fusion(bf16[512,4096]{1,0:T(8,128)(2,1)S(1)} %copy-done.10, bf16[1024,4608]{1,0:T(8,128)(2,1)} %all-gather.2.cloned.1.call-done, s32[1024]{0:T(1024)S(1)} %lt.44, s32[1024]{0:T(1024)S(1)} %ge.18), kind=kOutput, calls=%fused_computation.20 | convolution fusion | flops 4297064448 | bytes 14688256 | tf_op jit(solution)/shard_map/dot_general | solution.py:52
  193.6 1.3 collective-permute-start.3
  195.2 6.8 %fusion.9 = f32[4096,512]{0,1:T(8,128)} fusion(bf16[512,512]{1,0:T(8,128)(2,1)} %param.12, bf16[8192,512]{1,0:T(8,128)(2,1)S(1)} %bitcast.91, s32[]{:T(128)S(6)} %select_n.49), kind=kOutput, calls=%fused_computation.14 | convolution fusion | flops 2147483648 | bytes 13107204 | tf_op jit(solution)/shard_map/dot_general | solution.py:52
  202.0 5.0 %collective-permute-done.3 = f32[512,256]{0,1:T(8,128)S(1)} collective-permute-done((f32[512,256]{0,1:T(8,128)S(1)}, f32[512,256]{0,1:T(8,128)S(1)}, u32[]{:S(2)}, u32[]{:S(2)}) %collective-permute-start.3) | collective-permute-done | bytes 524320 | tf_op jit(solution)/shard_map/ppermute | solution.py:129
  207.1 1.7 bitcast_select_fusion.2
  208.7 23.8 %all-to-all-done = bf16[16,48,4608]{2,1,0:T(8,128)(2,1)} async-done(((bf16[16,48,4608]{2,1,0:T(8,128)(2,1)}), bf16[16,48,4608]{2,1,0:T(8,128)(2,1)}, u32[]{:S(2)}, u32[]{:S(2)}) %all-to-all-start) | async-done | bytes 7077920 | tf_op jit(solution)/shard_map/all_to_all | solution.py:89
  232.6 10.5 %fusion.1 = f32[512,4096]{1,0:T(8,128)} fusion(bf16[512,1024]{0,1:T(8,128)(2,1)S(1)} %get-tuple-element.16, bf16[1024,4608]{1,0:T(8,128)(2,1)} %all-gather.2.cloned.1.call-done), kind=kOutput, calls=%fused_computation.3 | convolution fusion | flops 4294967296 | bytes 17825792 | tf_op jit(solution)/shard_map/dot_general | solution.py:52
  243.1 1.5 convolution_multiply_fusion.1
  244.6 5.0 %fusion.7 = f32[768,64]{0,1:T(8,128)S(1)} fusion(bf16[64,4096]{1,0:T(8,128)(2,1)S(1)} %copy-done.4, bf16[768,4608]{1,0:T(8,128)(2,1)} %bitcast.8), kind=kOutput, calls=%fused_computation.11 | convolution fusion | flops 402653184 | bytes 7012352 | tf_op jit(solution)/shard_map/dot_general | solution.py:52
  249.6 1.3 collective-permute-start.5
  250.9 9.6 %fusion = bf16[512,4096]{1,0:T(8,128)(2,1)} fusion(f32[512,4096]{1,0:T(8,128)} %fusion.1, f32[4096,512]{0,1:T(8,128)S(1)} %bitcast.88, bf16[512,512]{1,0:T(8,128)(2,1)} %collective-permute-done.4, bf16[2048,512]{1,0:T(8,128)(2,1)S(1)} %copy-done.1, bf16[2048,512]{1,0:T(8,128)(2,1)S(1)} %get-tuple-element.36), kind=kOutput, calls=%fused_computation.1 | convolution fusion | flops 2162163712 | bytes 25690112 | tf_op jit(solution)/shard_map/dot_general | solution.py:52
  260.5 2.1 convolution_multiply_fusion
  264.0 2.2 fusion.42
  266.2 6.8 %fusion.36 = (f32[1,64,4096]{2,1,0:T(8,128)}, f32[1,64,4096]{2,1,0:T(8,128)}, f32[1,64,4096]{2,1,0:T(8,128)}) fusion(f32[1,64,4096]{2,1,0:T(8,128)} %param.19, f32[1,64,4096]{2,1,0:T(8,128)} %param.18, f32[1,64,4096]{2,1,0:T(8,128)S(1)} %copy-done.6, bf16[768,4608]{1,0:T(8,128)(2,1)} %bitcast.8, bf16[768,128]{0,1:T(8,128)(2,1)S(1)} %add_convert_fusion.2), kind=kOutput, calls=%fused_computation.58 | convolution fusion | flops 405798912 | bytes 12681216 | tf_op jit(solution)/shard_map/dot_general | solution.py:52
  (63 shorter events, 7.8 us)
Async XLA Ops:
  7.2 175.7 %all-gather.2.cloned.1.call-start = ((), (), s32[]{:S(2)}) async-start(), calls=%async_computation.1 | async-start | bytes 10027008 | tf_op jit(solution)/shard_map/all_gather | solution.py:95
  9.4 0.8 copy-start.3
  29.2 203.4 %all-to-all-start = ((bf16[16,48,4608]{2,1,0:T(8,128)(2,1)}), bf16[16,48,4608]{2,1,0:T(8,128)(2,1)}, u32[]{:S(2)}, u32[]{:S(2)}) async-start(bf16[16,48,4608]{2,1,0:T(8,128)(2,1)} %bitcast.89), calls=%async_computation | async-start | bytes 14155776 | tf_op jit(solution)/shard_map/all_to_all | solution.py:89
  37.5 46.9 %collective-permute-start = (bf16[2048,512]{1,0:T(8,128)(2,1)S(1)}, bf16[2048,512]{1,0:T(8,128)(2,1)S(1)}, u32[]{:S(2)}, u32[]{:S(2)}) collective-permute-start(bf16[2048,512]{1,0:T(8,128)(2,1)S(1)} %constant_dynamic-slice_fusion), channel_id=1, source_target_pairs={{0,1},{1,0},{2,3},{3,2},{4,5},{5,4},{6,7},{7,6},{8,9},{9,8},{10,11... | collective-permute-start | bytes 6291464 | tf_op jit(solution)/shard_map/ppermute | solution.py:102
  84.4 1.3 copy-start.5
  84.4 5.1 %collective-permute-start.1 = (bf16[2048,512]{1,0:T(8,128)(2,1)S(1)}, bf16[2048,512]{1,0:T(8,128)(2,1)}, u32[]{:S(2)}, u32[]{:S(2)}) collective-permute-start(bf16[2048,512]{1,0:T(8,128)(2,1)S(1)} %collective-permute-done), channel_id=1, source_target_pairs={{0,2},{2,0},{4,6},{6,4},{8,10},{10,8},{12,14},{14,12},{16,18},{18,... | collective-permute-start | bytes 6291464 | tf_op jit(solution)/shard_map/ppermute | solution.py:107
  85.7 6.3 %copy-start.9 = (bf16[512,4096]{1,0:T(8,128)(2,1)S(1)}, bf16[512,4096]{1,0:T(8,128)(2,1)}, u32[]{:S(2)}) copy-start(bf16[512,4096]{1,0:T(8,128)(2,1)} %param.11) | copy-start | bytes 12582916
  92.0 3.4 %copy-start = (bf16[2048,512]{1,0:T(8,128)(2,1)}, bf16[2048,512]{1,0:T(8,128)(2,1)S(1)}, u32[]{:S(2)}) copy-start(bf16[2048,512]{1,0:T(8,128)(2,1)S(1)} %get-tuple-element.37) | copy-start | bytes 6291460
  95.4 24.7 %collective-permute-start.2 = (f32[512,512]{0,1:T(8,128)}, f32[512,512]{0,1:T(8,128)S(1)}, u32[]{:S(2)}, u32[]{:S(2)}) collective-permute-start(f32[512,512]{0,1:T(8,128)} %fusion.18), channel_id=1, source_target_pairs={{0,1},{1,0},{2,3},{3,2},{4,5},{5,4},{6,7},{7,6},{8,9},{9,8},{10,11... | collective-permute-start | bytes 3145736 | tf_op jit(solution)/shard_map/ppermute | solution.py:117
  182.9 2.8 copy-start.10
  185.4 9.8 %slice-start.2 = ((s8[8388608]{0:T(1024)(128)(4,1)}), s8[4194304]{0:T(1024)(128)(4,1)S(1)}, s32[]{:S(2)}) async-start(s8[8388608]{0:T(1024)(128)(4,1)} %bitcast.90), calls=%async_computation.4 | async-start | bytes 8388608
  185.7 9.5 %slice-start.3 = ((s8[8388608]{0:T(1024)(128)(4,1)}), s8[4194304]{0:T(1024)(128)(4,1)S(1)}, s32[]{:S(2)}) async-start(s8[8388608]{0:T(1024)(128)(4,1)} %bitcast.90), calls=%async_computation.5 | async-start | bytes 8388608
  193.6 13.3 %collective-permute-start.3 = (f32[512,256]{0,1:T(8,128)S(1)}, f32[512,256]{0,1:T(8,128)S(1)}, u32[]{:S(2)}, u32[]{:S(2)}) collective-permute-start(f32[512,256]{0,1:T(8,128)S(1)} %pad_maximum_fusion.7), channel_id=1, source_target_pairs={{0,1},{1,0},{2,3},{3,2},{4,5},{5,4},{6,7},{7,6},{8,9},{9,8},{10,11... | collective-permute-start | bytes 1572872 | tf_op jit(solution)/shard_map/ppermute | solution.py:129
  194.9 56.0 %collective-permute-start.4 = (bf16[512,512]{1,0:T(8,128)(2,1)}, bf16[512,512]{1,0:T(8,128)(2,1)}, u32[]{:S(2)}, u32[]{:S(2)}) collective-permute-start(bf16[512,512]{1,0:T(8,128)(2,1)} %param.12), channel_id=1, source_target_pairs={{0,1},{1,0},{2,3},{3,2},{4,5},{5,4},{6,7},{7,6},{8,9},{9,8},{10,11... | collective-permute-start | bytes 1572872 | tf_op jit(solution)/shard_map/ppermute | solution.py:100
  232.6 18.3 %slice-start = ((s8[8388608]{0:T(1024)(128)(4,1)}), s8[4194304]{0:T(1024)(128)(4,1)S(1)}, s32[]{:S(2)}) async-start(s8[8388608]{0:T(1024)(128)(4,1)} %bitcast.87), calls=%async_computation.2 | async-start | bytes 8388608
  232.6 12.0 %copy-start.4 = (bf16[64,4096]{1,0:T(8,128)(2,1)S(1)}, bf16[64,4096]{1,0:T(8,128)(2,1)}, u32[]{:S(2)}) copy-start(bf16[64,4096]{1,0:T(8,128)(2,1)} %copy-done.3) | copy-start | bytes 1572868
  232.6 18.3 %slice-start.1 = ((s8[8388608]{0:T(1024)(128)(4,1)}), s8[4194304]{0:T(1024)(128)(4,1)S(1)}, s32[]{:S(2)}) async-start(s8[8388608]{0:T(1024)(128)(4,1)} %bitcast.87), calls=%async_computation.3 | async-start | bytes 8388608
  244.6 6.3 %copy-start.1 = (bf16[2048,512]{1,0:T(8,128)(2,1)S(1)}, bf16[2048,512]{1,0:T(8,128)(2,1)}, u32[]{:S(2)}) copy-start(bf16[2048,512]{1,0:T(8,128)(2,1)} %copy-done) | copy-start | bytes 6291460
  249.6 10.9 %copy-start.7 = (bf16[512,1024]{0,1:T(8,128)(2,1)S(1)}, bf16[512,1024]{0,1:T(8,128)(2,1)}, u32[]{:S(2)}) copy-start(bf16[512,1024]{0,1:T(8,128)(2,1)} %get-tuple-element.15) | copy-start | bytes 3145732
  249.6 14.3 %collective-permute-start.5 = (f32[768,128]{0,1:T(8,128)S(1)}, f32[768,128]{0,1:T(8,128)S(1)}, u32[]{:S(2)}, u32[]{:S(2)}) collective-permute-start(f32[768,128]{0,1:T(8,128)S(1)} %pad_maximum_fusion.8), channel_id=1, source_target_pairs={{0,1},{1,0},{2,3},{3,2},{4,5},{5,4},{6,7},{7,6},{8,9},{9,8},{10,11... | collective-permute-start | bytes 1179656 | tf_op jit(solution)/shard_map/ppermute | solution.py:146
  260.5 2.1 copy-start.2
  260.5 3.5 %copy-start.8 = (f32[1,64,512]{2,1,0:T(8,128)S(1)}, f32[1,64,512]{2,1,0:T(8,128)}, u32[]{:S(2)}) copy-start(f32[1,64,512]{2,1,0:T(8,128)} %param.17) | copy-start | bytes 393220
  260.5 3.5 %copy-start.11 = (f32[1,64,512]{2,1,0:T(8,128)S(1)}, f32[1,64,512]{2,1,0:T(8,128)}, u32[]{:S(2)}) copy-start(f32[1,64,512]{2,1,0:T(8,128)} %param.21) | copy-start | bytes 393220
  260.5 3.5 %copy-start.12 = (f32[1,64,512]{2,1,0:T(8,128)S(1)}, f32[1,64,512]{2,1,0:T(8,128)}, u32[]{:S(2)}) copy-start(f32[1,64,512]{2,1,0:T(8,128)} %param.20) | copy-start | bytes 393220
  262.7 3.6 %copy-start.6 = (f32[1,64,4096]{2,1,0:T(8,128)S(1)}, f32[1,64,4096]{2,1,0:T(8,128)}, u32[]{:S(2)}) copy-start(f32[1,64,4096]{2,1,0:T(8,128)} %param.16) | copy-start | bytes 3145732
Sparse Core Ops, SparseCore 0:
  11.2 171.6 all-gather.1
